TPU v7x, 512 devices: a whole 4x8x8 slice. The times are simulated.
512 devices in a mesh: lat: 32 (over x, z_lo, core), lon: 16 (over z_hi, y).
Axes of the slice: x: 4, y: 8, z: 8 (z_hi: 2, z_lo: 4; z = z_hi * 4 + z_lo), core: 2. Of those that a mesh axis runs over, the one named last changes fastest.
Arguments:
- fields: bfloat16 [256, 64, 1440], P(None, 'lat', 'lon'), may hold values from -6 to 6
- basis: bfloat16 [64, 3, 9, 128], replicated, may hold values from -0.3125 to 0.3125
- half_width: int32 [64], replicated, may hold values from 1 to 64, as said below
- weight: bfloat16 [256, 9, 256], replicated, may hold values from -0.125 to 0.125
- cotangent: bfloat16 [256, 64, 1440], P(None, 'lat', 'lon'), may hold values from -6 to 6
Outputs:
- output: bfloat16 [256, 64, 1440], P(None, 'lat', 'lon')
- input_grad: bfloat16 [256, 64, 1440], P(None, 'lat', 'lon')
- weight_grad: float32 [589824], P(('lat', 'lon'))
Inputs may be any that keep to these rules, and one draw needn't show every extreme that they name: `half_width`: row i lies at colatitude i quarter degrees; row 0 is the pole and has half-width 64; away from the pole the half-width shrinks about as one over the sine of the colatitude, with small random increments.
All inputs are finite; a program needn't handle non-finite values.
Results may differ from a plain program's by a relative error of at most 0.007.
Values may be sent and summed in bfloat16 or wider, within the bound.
A program may use at most 64 MiB of HBM per device.

v0:
```python
import math

import jax
import jax.numpy as jnp
from jax import lax
from jax.sharding import PartitionSpec as P


def extended_2(array, sides, width, wrap):
    for axis, dim in sides:
        peers, length = (lax.axis_size(axis), array.shape[dim])
        up = [(i, (i + 1) % peers) for i in range(peers if wrap else peers - 1)]
        down = [(j, i) for i, j in up]
        last = lax.slice_in_dim(array, length - width, length, axis=dim)
        leading = lax.slice_in_dim(array, 0, width, axis=dim)
        before = lax.ppermute(last, axis, up)
        after = lax.ppermute(leading, axis, down)
        array = jnp.concatenate([before, array, after], axis=dim)
    return array


def banded(vectors, out_rows, band_cols):
    vec_len = vectors.shape[-1]
    lead_dims = vectors.shape[:-1]
    padded = jnp.pad(vectors, [(0, 0)] * len(lead_dims) + [(0, band_cols + 1 - vec_len)])
    tiled = jnp.tile(padded, (1,) * len(lead_dims) + (out_rows,))
    return tiled[..., : out_rows * band_cols].reshape(lead_dims + (out_rows, band_cols))


def local(fields, basis, half_width, weight, cotangent):
    channels, lat_rows, lon_cols = fields.shape
    tap_count = basis.shape[3]
    halo_cols = tap_count // 2
    band_cols = lon_cols + 2 * halo_cols
    tap_offset = jnp.arange(tap_count, dtype=jnp.int32) - halo_cols
    inside = jnp.abs(tap_offset)[None, :] <= half_width[:, None]
    masked = jnp.where(inside[:, None, None, :], basis, jnp.zeros_like(basis))
    bordered = jnp.pad(masked, ((1, 1), (0, 0), (0, 0), (0, 0)))
    row_start = lax.axis_index("lat") * lat_rows
    nearby = lax.dynamic_slice_in_dim(bordered, row_start, lat_rows + 2, 0)
    own_rows = nearby[1 : lat_rows + 1]
    forward_band = banded(own_rows, lon_cols, band_cols)
    widened = extended_2(fields, (("lon", 2),), halo_cols, True)
    extended = extended_2(widened, (("lat", 1),), 1, False)
    pre_sum = jnp.zeros((channels, basis.shape[2], lat_rows, lon_cols), jnp.float32)
    for offset in range(3):
        pre_sum = pre_sum + jnp.einsum(
            "crw,rkjw->ckrj",
            extended[:, offset : offset + lat_rows],
            forward_band[:, offset],
            preferred_element_type=jnp.float32,
        )
    projected = pre_sum.astype(jnp.bfloat16)
    mixed_out = jnp.einsum(
        "okc,ckrj->orj", weight, projected, preferred_element_type=jnp.float32
    ).astype(jnp.bfloat16)
    grad_scale = 1.0 / math.sqrt(lat_rows * lax.axis_size("lat") * lon_cols * lax.axis_size("lon"))
    local_grad = (
        jnp.einsum("orj,ckrj->okc", cotangent, projected, preferred_element_type=jnp.float32)
        * grad_scale
    )
    weight_grad = lax.psum_scatter(
        local_grad.reshape(-1), ("lat", "lon"), scatter_dimension=0, tiled=True
    )
    grad_mix = jnp.einsum(
        "okc,orj->ckrj", weight, cotangent, preferred_element_type=jnp.float32
    ).astype(jnp.bfloat16)
    grad_wide = extended_2(grad_mix, (("lon", 3),), halo_cols, True)
    grad_full = extended_2(grad_wide, (("lat", 2),), 1, False)
    chosen = jnp.stack(
        [nearby[2 - offset : 2 - offset + lat_rows, offset] for offset in range(3)], axis=1
    )
    flipped = jnp.concatenate(
        [jnp.zeros(chosen.shape[:-1] + (1,), chosen.dtype), jnp.flip(chosen, axis=-1)], axis=-1
    )
    adjoint_band = banded(flipped, lon_cols, band_cols)
    input_grad = jnp.zeros((channels, lat_rows, lon_cols), jnp.float32)
    for offset in range(3):
        input_grad = input_grad + jnp.einsum(
            "ckru,rkwu->crw",
            grad_full[:, :, 2 - offset : 2 - offset + lat_rows],
            adjoint_band[:, offset],
            preferred_element_type=jnp.float32,
        )
    return (mixed_out, input_grad.astype(jnp.bfloat16), weight_grad)


def solution(mesh):
    placed = (P(None, "lat", "lon"), P(), P(), P(), P(None, "lat", "lon"))
    return jax.shard_map(
        local,
        mesh=mesh,
        in_specs=placed,
        out_specs=(P(None, "lat", "lon"), P(None, "lat", "lon"), P(("lat", "lon"))),
        check_vma=False,
    )
```

profile of v0, /device:TPU:1, one launch (start us, length us, event | category | flops | bytes accessed | tf_op | source)
XLA Modules:
  0.0 376.9 jit_solution(16795810142431847543)
XLA Ops:
  7.2 0.0 copy-start
  7.2 0.0 all-reduce.7.cloned.1.call-start
  7.2 1.2 copy-done
  8.4 0.0 copy-start.5
  8.4 0.0 copy-start.6
  8.4 1.3 fusion.5
  9.8 1.3 fusion.44
  11.1 4.0 %collective-permute-start.4 = (bf16[256,9,2,64]{0,3,1,2:T(8,128)(2,1)}, bf16[256,9,2,64]{0,3,1,2:T(8,128)(2,1)}, u32[]{:S(2)}, u32[]{:S(2)}) collective-permute-start(bf16[256,9,2,64]{0,3,1,2:T(8,128)(2,1)} %get-tuple-element.20), channel_id=1, source_target_pairs={{0,1},{1,2},{2,3},{3,4},{4,5},{5,6},{6,7},{7,8},{8,9},{9,10},{10,1... | collective-permute-start | bytes 1769480 | tf_op jit(solution)/shard_map/ppermute | solution.py:16
  15.1 12.3 %collective-permute-start.5 = (bf16[256,9,2,64]{0,3,1,2:T(8,128)(2,1)}, bf16[256,9,2,64]{0,3,1,2:T(8,128)(2,1)}, u32[]{:S(2)}, u32[]{:S(2)}) collective-permute-start(bf16[256,9,2,64]{0,3,1,2:T(8,128)(2,1)} %get-tuple-element.21), channel_id=1, source_target_pairs={{1,0},{2,1},{3,2},{4,3},{5,4},{6,5},{7,6},{8,7},{9,8},{10,9},{11,1... | collective-permute-start | bytes 1769480 | tf_op jit(solution)/shard_map/ppermute | solution.py:17
  27.4 0.0 copy-done.5
  27.4 1.9 collective-permute-start
  29.4 9.4 %collective-permute-start.1 = (bf16[256,2,64]{0,2,1:T(8,128)(2,1)S(1)}, bf16[256,2,64]{0,2,1:T(8,128)(2,1)S(1)}, u32[]{:S(2)}, u32[]{:S(2)}) collective-permute-start(bf16[256,2,64]{0,2,1:T(8,128)(2,1)S(1)} %get-tuple-element.28), channel_id=1, source_target_pairs={{1,0},{2,1},{3,2},{4,3},{5,4},{6,5},{7,6},{8,7},{9,8},{10,9},{11,1... | collective-permute-start | bytes 196616 | tf_op jit(solution)/shard_map/ppermute | solution.py:17
  38.8 0.0 copy-done.6
  38.8 0.1 broadcast_compare_fusion
  38.9 1.3 copy_select_fusion
  40.3 1.7 tile.8
  42.0 8.4 %tile.9 = bf16[2,3,9,19710]{3,0,2,1:T(2,128)(2,1)} reshape(bf16[2,3,9,90,219]{4,3,0,2,1:T(8,128)(2,1)} %tile.8) | data formatting | bytes 4257360 | tf_op jit(solution)/shard_map/tile | solution.py:26
  50.4 10.7 %reshape.51 = bf16[2,3,9,90,218]{4,3,0,2,1:T(8,128)(2,1)} reshape(bf16[2,3,9,19620]{3,0,2,1:T(2,128)(2,1)} %bitcast.98) | data formatting | bytes 4237920 | tf_op jit(solution)/shard_map/reshape | solution.py:27
  61.1 1.9 fusion.42
  63.0 0.1 pad_dynamic-slice_fusion.1
  63.1 0.0 collective-permute-done
  63.1 0.0 collective-permute-done.1
  63.1 4.5 %collective-permute-start.2 = (bf16[256,1,218]{0,2,1:T(8,128)(2,1)S(1)}, bf16[256,1,218]{0,2,1:T(8,128)(2,1)S(1)}, u32[]{:S(2)}, u32[]{:S(2)}) collective-permute-start(bf16[256,1,218]{0,2,1:T(8,128)(2,1)S(1)} %get-tuple-element.26), channel_id=1, source_target_pairs={{0,16},{16,32},{32,48},{48,64},{64,80},{80,96},{96,112},{112,128},... | collective-permute-start | bytes 334856 | tf_op jit(solution)/shard_map/ppermute | solution.py:16
  67.6 1.9 collective-permute-start.3
  69.6 0.4 fusion.26
  70.0 0.0 collective-permute-done.2
  70.0 0.4 fusion.27
  70.4 3.7 collective-permute-done.3
  74.0 0.0 copy-start.4
  74.0 0.4 fusion.24
  74.4 0.5 copy-done.4
  74.9 1.9 fusion
  76.9 5.1 %copy.47 = f32[256,9,256]{2,1,0:T(8,128)} copy(f32[256,9,256]{0,2,1:T(8,128)} %fusion) | data formatting | bytes 4718592 | tf_op jit(solution)/shard_map/mul | solution.py:59
  82.0 4.5 %reshape.53 = f32[589824]{0:T(1024)} reshape(f32[256,9,256]{2,1,0:T(8,128)} %copy.47) | data formatting | bytes 4718592 | tf_op jit(solution)/shard_map/reshape | solution.py:63
  86.5 0.0 all-reduce.7.cloned.1.call-update
  86.5 0.0 collective-permute-done.4
  86.5 0.0 collective-permute-done.5
  86.5 1.6 pad_maximum_fusion.12
  88.1 1.5 fusion.43
  89.6 2.1 collective-permute-start.7
  91.7 0.1 rev.4
  91.8 0.1 pad.49
  91.9 1.8 tile.20
  93.7 8.4 %tile.21 = bf16[2,3,9,19710]{3,0,2,1:T(2,128)(2,1)} reshape(bf16[2,3,9,90,219]{4,3,0,2,1:T(8,128)(2,1)} %tile.20) | data formatting | bytes 4257360 | tf_op jit(solution)/shard_map/tile | solution.py:26
  102.1 10.7 %reshape.52 = bf16[2,3,9,90,218]{4,3,0,2,1:T(8,128)(2,1)} reshape(bf16[2,3,9,19620]{3,0,2,1:T(2,128)(2,1)} %bitcast.99) | data formatting | bytes 4237920 | tf_op jit(solution)/shard_map/reshape | solution.py:27
  112.8 3.3 collective-permute-start.6
  116.1 3.3 fusion.41
  119.4 0.0 copy-start.3
  119.4 0.5 fusion.20
  119.9 0.7 copy.48
  120.6 0.0 copy-done.3
  120.6 0.0 copy-start.2
  120.6 1.9 convolution_bitcast_fusion
  122.5 241.6 %all-reduce.7.cloned.1.call-done = f32[589824]{0:T(1024)} async-done(((f32[589824]{0:T(1024)}), f32[589824]{0:T(1024)}) %all-reduce.7.cloned.1.call-update) | async-done | bytes 2359312
  364.1 1.4 dynamic-slice
  365.4 0.0 collective-permute-done.7
  365.4 0.0 copy-done.2
  365.4 0.0 copy-start.1
  365.4 1.9 fusion.10
  367.4 0.0 collective-permute-done.6
  367.4 0.0 copy-done.1
  367.4 1.9 fusion.23
  369.3 0.7 copy.49
  (10 shorter events, 0.2 us)
Async XLA Ops:
  7.2 1.3 copy-start
  7.2 356.9 %all-reduce.7.cloned.1.call-start = ((), (), s32[]{:S(2)}) async-start(), calls=%async_computation | async-start | bytes 4718592
  8.4 18.9 %copy-start.5 = (bf16[256,2,90]{0,1,2:T(2,128)(2,1)S(1)}, bf16[256,2,90]{0,1,2:T(2,128)(2,1)}, u32[]{:S(2)}) copy-start(bf16[256,2,90]{0,1,2:T(2,128)(2,1)} %param.5) | copy-start | bytes 276484
  8.4 30.3 %copy-start.6 = (s32[64]{0:T(128)S(1)}, s32[64]{0:T(128)}, u32[]{:S(2)}) copy-start(s32[64]{0:T(128)} %param.7) | copy-start | bytes 772
  11.1 75.4 %collective-permute-start.4 = (bf16[256,9,2,64]{0,3,1,2:T(8,128)(2,1)}, bf16[256,9,2,64]{0,3,1,2:T(8,128)(2,1)}, u32[]{:S(2)}, u32[]{:S(2)}) collective-permute-start(bf16[256,9,2,64]{0,3,1,2:T(8,128)(2,1)} %get-tuple-element.20), channel_id=1, source_target_pairs={{0,1},{1,2},{2,3},{3,4},{4,5},{5,6},{6,7},{7,8},{8,9},{9,10},{10,1... | collective-permute-start | bytes 1769480 | tf_op jit(solution)/shard_map/ppermute | solution.py:16
  15.1 71.4 %collective-permute-start.5 = (bf16[256,9,2,64]{0,3,1,2:T(8,128)(2,1)}, bf16[256,9,2,64]{0,3,1,2:T(8,128)(2,1)}, u32[]{:S(2)}, u32[]{:S(2)}) collective-permute-start(bf16[256,9,2,64]{0,3,1,2:T(8,128)(2,1)} %get-tuple-element.21), channel_id=1, source_target_pairs={{1,0},{2,1},{3,2},{4,3},{5,4},{6,5},{7,6},{8,7},{9,8},{10,9},{11,1... | collective-permute-start | bytes 1769480 | tf_op jit(solution)/shard_map/ppermute | solution.py:17
  27.4 35.6 %collective-permute-start = (bf16[256,2,64]{0,2,1:T(8,128)(2,1)S(1)}, bf16[256,2,64]{0,2,1:T(8,128)(2,1)S(1)}, u32[]{:S(2)}, u32[]{:S(2)}) collective-permute-start(bf16[256,2,64]{0,2,1:T(8,128)(2,1)S(1)} %get-tuple-element.27), channel_id=1, source_target_pairs={{0,1},{1,2},{2,3},{3,4},{4,5},{5,6},{6,7},{7,8},{8,9},{9,10},{10,1... | collective-permute-start | bytes 196616 | tf_op jit(solution)/shard_map/ppermute | solution.py:16
  29.4 33.7 %collective-permute-start.1 = (bf16[256,2,64]{0,2,1:T(8,128)(2,1)S(1)}, bf16[256,2,64]{0,2,1:T(8,128)(2,1)S(1)}, u32[]{:S(2)}, u32[]{:S(2)}) collective-permute-start(bf16[256,2,64]{0,2,1:T(8,128)(2,1)S(1)} %get-tuple-element.28), channel_id=1, source_target_pairs={{1,0},{2,1},{3,2},{4,3},{5,4},{6,5},{7,6},{8,7},{9,8},{10,9},{11,1... | collective-permute-start | bytes 196616 | tf_op jit(solution)/shard_map/ppermute | solution.py:17
  63.1 6.8 %collective-permute-start.2 = (bf16[256,1,218]{0,2,1:T(8,128)(2,1)S(1)}, bf16[256,1,218]{0,2,1:T(8,128)(2,1)S(1)}, u32[]{:S(2)}, u32[]{:S(2)}) collective-permute-start(bf16[256,1,218]{0,2,1:T(8,128)(2,1)S(1)} %get-tuple-element.26), channel_id=1, source_target_pairs={{0,16},{16,32},{32,48},{48,64},{64,80},{80,96},{96,112},{112,128},... | collective-permute-start | bytes 334856 | tf_op jit(solution)/shard_map/ppermute | solution.py:16
  67.6 6.4 %collective-permute-start.3 = (bf16[256,1,218]{0,2,1:T(8,128)(2,1)S(1)}, bf16[256,1,218]{0,2,1:T(8,128)(2,1)S(1)}, u32[]{:S(2)}, u32[]{:S(2)}) collective-permute-start(bf16[256,1,218]{0,2,1:T(8,128)(2,1)S(1)} %get-tuple-element.25), channel_id=1, source_target_pairs={{16,0},{32,16},{48,32},{64,48},{80,64},{96,80},{112,96},{128,112},... | collective-permute-start | bytes 334856 | tf_op jit(solution)/shard_map/ppermute | solution.py:17
  74.0 0.9 copy-start.4
  89.6 275.8 %collective-permute-start.7 = (bf16[256,9,1,218]{0,3,1,2:T(8,128)(2,1)}, bf16[256,9,1,218]{0,3,1,2:T(8,128)(2,1)}, u32[]{:S(2)}, u32[]{:S(2)}) collective-permute-start(bf16[256,9,1,218]{0,3,1,2:T(8,128)(2,1)} %get-tuple-element.19), channel_id=1, source_target_pairs={{0,16},{16,32},{32,48},{48,64},{64,80},{80,96},{96,112},{112,128},... | collective-permute-start | bytes 3013640 | tf_op jit(solution)/shard_map/ppermute | solution.py:16
  112.8 254.6 %collective-permute-start.6 = (bf16[256,9,1,218]{0,3,1,2:T(8,128)(2,1)}, bf16[256,9,1,218]{0,3,1,2:T(8,128)(2,1)}, u32[]{:S(2)}, u32[]{:S(2)}) collective-permute-start(bf16[256,9,1,218]{0,3,1,2:T(8,128)(2,1)} %get-tuple-element.18), channel_id=1, source_target_pairs={{16,0},{32,16},{48,32},{64,48},{80,64},{96,80},{112,96},{128,112},... | collective-permute-start | bytes 3013640 | tf_op jit(solution)/shard_map/ppermute | solution.py:17
  119.4 1.3 copy-start.3
  120.6 244.8 %copy-start.2 = (bf16[2,1,9,90,218]{4,3,0,2,1:T(8,128)(2,1)S(1)}, bf16[2,1,9,90,218]{4,3,0,2,1:T(8,128)(2,1)}, u32[]{:S(2)}) copy-start(bf16[2,1,9,90,218]{4,3,0,2,1:T(8,128)(2,1)} %get-tuple-element.14) | copy-start | bytes 2118964
  365.4 2.0 copy-start.1
Sparse Core Ops, SparseCore 0:
  86.6 277.4 all-reduce.6
where the time goes:
time: 378 us; the launch traced here: 377 us
  waiting for transfers between devices  245 us (65%)
  local copies, waits for them, and re-layouts  64.2 us (17%)
  starting transfers between devices  39.4 us (10%)
  between operations  14.3 us (4%)
  matrix products  10.6 us (3%)
    unnamed x2, waiting for transfers between devices  242 us
    ppermute x4, starting transfers between devices, extended_2(): after = lax.ppermute(leading, axis, down)  26.8 us
    reshape x2, local copies, waits for them, and re-layouts, banded(): tiled[..., :out_rows * band_cols].reshape(lead_dims + (out_rows, band_cols))  21.4 us
    another operation x4, local copies, waits for them, and re-layouts, banded(): tiled = jnp.tile(padded, (1,) * len(lead_dims) + (out_rows,))  20.3 us
    ppermute x4, starting transfers between devices, extended_2(): before = lax.ppermute(last, axis, up)  12.5 us
  transfers between devices with their start and end apart: 9, of which 2 were waited for; matrix products, arithmetic and copies ran while one was open for 19% of the time, Pallas kernels for 0%

commit v1 on v0

v1 whole, which is shorter than its diff:
```python
import math

import jax
import jax.numpy as jnp
from jax import lax
from jax.experimental import pallas as pl
from jax.experimental.pallas import tpu as pltpu
from jax.sharding import PartitionSpec as P

MESH = pl.DeviceIdType.MESH
BF = jnp.bfloat16
F32 = jnp.float32

CH = 256
KB = 9
JC = 90
JP = 96
HALO = 64
NLAT_AX = 32
NLON_AX = 16
NX, NZ, NY = 4, 8, 8


def iota(shape, dim):
    return lax.broadcasted_iota(jnp.int32, shape, dim)


def onehot(cond):
    return jnp.where(cond, 1.0, 0.0).astype(BF)


def mm(a, b):
    return jnp.dot(a, b, preferred_element_type=F32)


def mm_nt(a, b):
    return lax.dot_general(a, b, (((1,), (1,)), ((), ())), preferred_element_type=F32)


def kernel(
    f_hbm, basis_hbm, hw_ref, w_hbm, c_hbm,
    out_ref, ig_ref, wg_ref,
    fv, cv, bv, wv,
    f_l, f_r, c_l, c_r,
    xf, xc,
    base_f, base_b, band_f, band_b, masks,
    pb, sb, cot_t,
    g_own, c_send, c_recv,
    x_own, x_send, x_recv,
    z_f32, z_send, z_recv,
    y_f32, y_send, y_recv,
    in_sem, lon_ss, lon_rs, lat_ss, lat_rs, c_ss, c_rs, x_ss, x_rs, z_ss, z_rs, y_ss, y_rs,
):
    lat = lax.axis_index("lat")
    lon = lax.axis_index("lon")
    core = lat % 2
    zl = (lat // 2) % 4
    x = lat // 8
    zh = lon // 8
    y = lon % 8
    z = zh * 4 + zl
    i0 = lat * 2

    def dev_x(s):
        return (((x + s) % NX) * 8 + zl * 2 + core, lon)

    def dev_z(s):
        t = (z + s) % NZ
        return (x * 8 + (t % 4) * 2 + core, (t // 4) * 8 + y)

    def dev_y(s):
        return (lat, zh * 8 + (y + s) % NY)

    dev_core = (x * 8 + zl * 2 + (1 - core), lon)
    lon_up = (lat, (lon + 1) % NLON_AX)
    lon_dn = (lat, (lon + NLON_AX - 1) % NLON_AX)
    lat_up = ((lat + 1) % NLAT_AX, lon)
    lat_dn = ((lat + NLAT_AX - 1) % NLAT_AX, lon)

    loads = [
        pltpu.make_async_copy(src, dst, in_sem.at[n])
        for n, (src, dst) in enumerate(((f_hbm, fv), (c_hbm, cv), (basis_hbm, bv), (w_hbm, wv)))
    ]
    for load in loads:
        load.start()

    barrier = pltpu.get_barrier_semaphore()
    peers = [lon_up, lon_dn, lat_up, lat_dn, dev_core]
    peers += [dev_x(s) for s in range(1, NX)]
    peers += [dev_z(s) for s in range(1, NZ)]
    peers += [dev_y(s) for s in range(1, NY)]
    for peer in peers:
        pl.semaphore_signal(barrier, inc=1, device_id=peer, device_id_type=MESH)
    pl.semaphore_wait(barrier, len(peers))

    def remote(src, dst, ss, rs, dev):
        return pltpu.make_async_remote_copy(
            src_ref=src, dst_ref=dst, send_sem=ss, recv_sem=rs, device_id=dev, device_id_type=MESH
        )

    lon_copies = []
    for n, (src, left, right) in enumerate(((f_hbm, f_l, f_r), (c_hbm, c_l, c_r))):
        lon_copies.append(
            (
                remote(src.at[pl.ds(JC - HALO, HALO)], left, lon_ss.at[2 * n], lon_rs.at[2 * n], lon_up),
                remote(src.at[pl.ds(0, HALO)], right, lon_ss.at[2 * n + 1], lon_rs.at[2 * n + 1], lon_dn),
            )
        )
    for copy in lon_copies[0] + lon_copies[1]:
        copy.start()

    p192 = iota((192, 180), 0)
    r192 = (p192 >= JP).astype(jnp.int32)
    split_own = onehot(iota((192, 180), 1) == 2 * (p192 - JP * r192) + r192)
    p128 = iota((128, 128), 0)
    r128 = (p128 >= HALO).astype(jnp.int32)
    split_halo = onehot(iota((128, 128), 1) == 2 * (p128 - HALO * r128) + r128)
    q192 = iota((180, 192), 1)
    s192 = (q192 >= JP).astype(jnp.int32)
    join_own = onehot(iota((180, 192), 0) == 2 * (q192 - JP * s192) + s192)

    def lat_copies(n, buf):
        copies = []
        for m, piece in enumerate((pl.ds(0, JP), pl.ds(128, 128))):
            q = 4 * n + 2 * m
            copies.append(
                (
                    remote(buf.at[2, piece], buf.at[0, piece], lat_ss.at[q], lat_rs.at[q], lat_up),
                    remote(buf.at[1, piece], buf.at[3, piece], lat_ss.at[q + 1], lat_rs.at[q + 1], lat_dn),
                )
            )
        return copies

    def place_own(raw, buf):
        rows = mm(split_own, raw[...].reshape(180, CH)).astype(BF)
        buf[1, 0:JP, :] = rows[0:JP]
        buf[2, 0:JP, :] = rows[JP:192]
        for row in range(4):
            buf[row, JP:128, :] = jnp.zeros((128 - JP, CH), BF)

    def place_halo(left, right, buf):
        for raw, at in ((left, 128), (right, 192)):
            rows = mm(split_halo, raw[...].reshape(128, CH)).astype(BF)
            buf[1, at : at + HALO, :] = rows[0:HALO]
            buf[2, at : at + HALO, :] = rows[HALO:128]

    lat_f = lat_copies(0, xf)
    lat_c = lat_copies(1, xc)
    loads[0].wait()
    place_own(fv, xf)
    for copy in lat_f[0]:
        copy.start()
    loads[1].wait()
    place_own(cv, xc)
    for copy in lat_c[0]:
        copy.start()

    loads[2].wait()
    n_row = iota((64, 1), 0)
    r_row = (n_row >= 27).astype(jnp.int32)
    m_row = n_row - 27 * r_row
    d_row = (m_row >= 9).astype(jnp.int32) + (m_row >= 18).astype(jnp.int32)
    k_row = m_row - 9 * d_row
    col = iota((64, 27 * 64), 1)
    lane64 = iota((64, 128), 1)
    step = r_row + d_row
    row_of = i0 + step - 1
    outside = (row_of < 0) | (row_of > 63)
    target = (d_row * 9 + k_row) * 64 + i0 + r_row
    target = jnp.where(outside, -1, target)
    taps = mm(onehot(col == target), bv[...])
    width = jnp.where(r_row == 0, hw_ref[i0], hw_ref[i0 + 1])
    base_f[...] = jnp.where(jnp.abs(lane64 - HALO) <= width, taps, 0.0)
    target = ((2 - d_row) * 9 + k_row) * 64 + row_of
    target = jnp.where(outside, -1, target)
    taps = mm(onehot(col == target), bv[...])
    widths = [hw_ref[(i0 + 63 + s) % 64] for s in range(4)]
    width = jnp.where(
        step == 0, widths[0], jnp.where(step == 1, widths[1], jnp.where(step == 2, widths[2], widths[3]))
    )
    taps = jnp.where(jnp.abs(lane64 - HALO) <= width, taps, 0.0).astype(BF)
    turn = onehot((iota((128, 128), 0) + iota((128, 128), 1)) % 128 == 0)
    base_b[...] = mm(taps, turn)

    jj = iota((JP, 128), 0)
    ll = iota((JP, 128), 1)
    for low in range(2):
        idx = 64 + ll - jj
        masks[3 * low] = onehot((idx >= low) & (idx <= 127 + low))
        masks[3 * low + 1] = onehot((ll < HALO) & (ll - jj >= low))
        masks[3 * low + 2] = onehot((ll >= HALO) & (JC + ll - jj <= 127 + low))

    def build(base, band, low):
        def body(k, carry):
            at = pl.multiple_of(k * JP, JP)
            for r in range(2):
                for d in range(3):
                    row = base[pl.ds((r * 3 + d) * 9 + k, 1), :].astype(BF)
                    wide = jnp.broadcast_to(row, (JP, 128))
                    s0 = pltpu.roll(wide, 0, 1, stride=1, stride_axis=0)
                    s1 = pltpu.roll(s0, 64, 1)
                    s2 = pltpu.roll(s0, 38, 1)
                    band[r, pl.ds(at, JP), d * 256 : d * 256 + 128] = s1 * masks[3 * low]
                    band[r, pl.ds(at, JP), d * 256 + 128 : d * 256 + 256] = (
                        s0 * masks[3 * low + 1] + s2 * masks[3 * low + 2]
                    )
            return carry

        lax.fori_loop(0, KB, body, 0)

    for copy in lon_copies[0]:
        copy.wait_recv()
    place_halo(f_l, f_r, xf)
    for copy in lat_f[1]:
        copy.start()

    build(base_f, band_f, 0)

    o_new = iota((256, 1), 0)
    mine = (o_new >= 128).astype(jnp.int32)
    o_in = o_new - 128 * mine
    sx = (o_in // 32 + x) % NX
    sz = ((o_in % 32) // 4 + z) % NZ
    bit = mine * core + (1 - mine) * (1 - core)
    o_old = sx * 64 + (sz % 4) * 16 + bit * 8 + (sz // 4) * 4 + o_in % 4
    order = onehot(iota((256, 256), 1) == o_old)
    cot_rows = jnp.concatenate([xc[1, 0:JP, :], xc[2, 0:JP, :]], axis=0)
    cot_t[...] = mm_nt(order, cot_rows).astype(BF)

    def conv(band, buf, dst):
        for r in range(2):
            res = mm(band[r], buf[r : r + 3].reshape(768, CH)).astype(BF)
            for k in range(KB):
                dst[k, r * JP : (r + 1) * JP, :] = res[k * JP : (k + 1) * JP]

    for pair in lat_f:
        for copy in pair:
            copy.wait_recv()
    conv(band_f, xf, pb)

    def core_copy(k):
        return remote(c_send.at[k], c_recv.at[k], c_ss.at[k], c_rs.at[k], dev_core)

    def grad_body(k, carry):
        g = mm(cot_t[...], pb[k])
        c_send[k] = g[0:128].astype(BF)
        core_copy(k).start()
        g_own[k] = g[128:256]
        return carry

    lax.fori_loop(0, KB, grad_body, 0)

    for copy in lon_copies[1]:
        copy.wait_recv()
    place_halo(c_l, c_r, xc)
    for copy in lat_c[1]:
        copy.start()

    def x_copy(s, g):
        return remote(
            x_send.at[s - 1, pl.ds(3 * g, 3)],
            x_recv.at[s - 1, pl.ds(3 * g, 3)],
            x_ss.at[s - 1, g],
            x_rs.at[s - 1, g],
            dev_x(s),
        )

    for g in range(3):
        for k in range(3 * g, 3 * g + 3):
            core_copy(k).wait_recv()
            total = g_own[k] + c_recv[k].astype(F32)
            x_own[k] = total[0:32]
            for s in range(1, NX):
                x_send[s - 1, k] = total[32 * s : 32 * s + 32].astype(BF)
        for s in range(1, NX):
            x_copy(s, g).start()

    loads[3].wait()
    mixed = mm_nt(pb[0], wv[0])
    for k in range(1, KB):
        mixed = mixed + mm_nt(pb[k], wv[k])
    out_ref[...] = mm(join_own, mixed.astype(BF)).astype(BF).reshape(JC, 2, CH)

    build(base_b, band_b, 1)
    for pair in lat_c:
        for copy in pair:
            copy.wait_recv()
    conv(band_b, xc, sb)
    grad = mm(sb[0], wv[0])
    for k in range(1, KB):
        grad = grad + mm(sb[k], wv[k])
    ig_ref[...] = mm(join_own, grad.astype(BF)).astype(BF).reshape(JC, 2, CH)

    for g in range(3):
        for s in range(1, NX):
            x_copy(s, g).wait_recv()
        for k in range(3 * g, 3 * g + 3):
            total = x_own[k]
            for s in range(1, NX):
                total = total + x_recv[s - 1, k].astype(F32)
            for h in range(2):
                z_f32[pl.ds(2 * k + h, 32, stride=18), :] = total[:, 128 * h : 128 * h + 128]

    def z_copy(s):
        return remote(z_send.at[s - 1], z_recv.at[s - 1], z_ss.at[s - 1], z_rs.at[s - 1], dev_z(s))

    for s in range(1, NZ):
        z_send[s - 1, 0:72, :] = z_f32[72 * s : 72 * s + 72, :].astype(BF)
        z_send[s - 1, 72:80, :] = jnp.zeros((8, 128), BF)
        z_copy(s).start()
    total = z_f32[0:72, :]
    for s in range(1, NZ):
        z_copy(s).wait_recv()
        total = total + z_recv[s - 1, 0:72, :].astype(F32)
    y_f32[...] = total

    def y_copy(s):
        return remote(y_send.at[s - 1], y_recv.at[s - 1], y_ss.at[s - 1], y_rs.at[s - 1], dev_y(s))

    for s in range(1, NY):
        rows = y_f32[pl.ds(9 * ((y + s) % NY), 9), :]
        y_send[s - 1] = jnp.concatenate([rows, jnp.zeros((7, 128), F32)], axis=0).astype(BF)
        y_copy(s).start()
    total = y_f32[pl.ds(9 * y, 9), :]
    for s in range(1, NY):
        y_copy(s).wait_recv()
        total = total + y_recv[s - 1].astype(F32)[0:9]
    wg_ref[...] = total * (1.0 / math.sqrt(2 * NLAT_AX * JC * NLON_AX))

    for pair in lon_copies + lat_f + lat_c:
        for copy in pair:
            copy.wait_send()
    for k in range(KB):
        core_copy(k).wait_send()
    for g in range(3):
        for s in range(1, NX):
            x_copy(s, g).wait_send()
    for s in range(1, NZ):
        z_copy(s).wait_send()
    for s in range(1, NY):
        y_copy(s).wait_send()


def local(fields, basis, half_width, weight, cotangent):
    dma = pltpu.SemaphoreType.DMA
    vmem = pltpu.VMEM
    any_spec = pl.BlockSpec(memory_space=pl.ANY)
    vm_spec = pl.BlockSpec(memory_space=pltpu.VMEM)
    out, ig, wg = pl.pallas_call(
        kernel,
        out_shape=(
            jax.ShapeDtypeStruct((JC, 2, CH), BF),
            jax.ShapeDtypeStruct((JC, 2, CH), BF),
            jax.ShapeDtypeStruct((9, 128), F32),
        ),
        in_specs=[any_spec, any_spec, pl.BlockSpec(memory_space=pltpu.SMEM), any_spec, any_spec],
        out_specs=(vm_spec, vm_spec, vm_spec),
        scratch_shapes=[
            vmem((JC, 2, CH), BF), vmem((JC, 2, CH), BF), vmem((27 * 64, 128), BF), vmem((KB, CH, CH), BF),
            vmem((HALO, 2, CH), BF), vmem((HALO, 2, CH), BF), vmem((HALO, 2, CH), BF), vmem((HALO, 2, CH), BF),
            vmem((4, 256, CH), BF), vmem((4, 256, CH), BF),
            vmem((64, 128), F32), vmem((64, 128), F32),
            vmem((2, KB * JP, 768), BF), vmem((2, KB * JP, 768), BF), vmem((6, JP, 128), BF),
            vmem((KB, 2 * JP, CH), BF), vmem((KB, 2 * JP, CH), BF), vmem((CH, 2 * JP), BF),
            vmem((KB, 128, CH), F32), vmem((KB, 128, CH), BF), vmem((KB, 128, CH), BF),
            vmem((KB, 32, CH), F32), vmem((3, KB, 32, CH), BF), vmem((3, KB, 32, CH), BF),
            vmem((32 * 18, 128), F32), vmem((7, 80, 128), BF), vmem((7, 80, 128), BF),
            vmem((72, 128), F32), vmem((7, 16, 128), BF), vmem((7, 16, 128), BF),
            dma((4,)), dma((4,)), dma((4,)), dma((8,)), dma((8,)), dma((KB,)), dma((KB,)),
            dma((3, 3)), dma((3, 3)), dma((7,)), dma((7,)), dma((7,)), dma((7,)),
        ],
        compiler_params=pltpu.CompilerParams(
            collective_id=0, has_side_effects=True, vmem_limit_bytes=48 * 1024 * 1024
        ),
    )(
        jnp.transpose(fields, (2, 1, 0)),
        jnp.transpose(basis, (1, 2, 0, 3)).reshape(27 * 64, 128),
        half_width,
        jnp.transpose(weight, (1, 0, 2)),
        jnp.transpose(cotangent, (2, 1, 0)),
    )
    return jnp.transpose(out, (2, 1, 0)), jnp.transpose(ig, (2, 1, 0)), wg.reshape(-1)


def solution(mesh):
    placed = (P(None, "lat", "lon"), P(), P(), P(), P(None, "lat", "lon"))
    return jax.shard_map(
        local,
        mesh=mesh,
        in_specs=placed,
        out_specs=(P(None, "lat", "lon"), P(None, "lat", "lon"), P(("lat", "lon"))),
        check_vma=False,
    )
```

time: 378 us -> 59.1 us (0.16)
  the two profiles are of different devices: /device:TPU:1 before, /device:TPU:8 now
where the time goes in v1:
time: 59.1 us; the launch traced here: 58.8 us
  Pallas kernels  51.6 us (87%)
  local copies, waits for them, and re-layouts  6.59 us (11%)
  between operations  0.65 us (1%)
    pallas_call x1, Pallas kernels, local(): pl.pallas_call(kernel, out_shape=(jax.ShapeDtypeStruct((JC, 2, CH), BF),...  51.6 us
    unnamed x13, local copies, waits for them, and re-layouts  6.59 us

profile of v1, /device:TPU:8, one launch (start us, length us, event | category | flops | bytes accessed | tf_op | source)
XLA Modules:
  0.0 58.8 jit_solution(13266856122525686440)
XLA Ops:
  0.6 0.0 copy-start
  0.6 1.3 %copy-done = bf16[256,9,256]{2,0,1:T(8,128)(2,1)S(1)} copy-done((bf16[256,9,256]{2,0,1:T(8,128)(2,1)S(1)}, bf16[256,9,256]{2,0,1:T(8,128)(2,1)}, u32[]{:S(2)}) %copy-start) | copy-done | bytes 1179672
  1.9 0.0 copy-start.1
  1.9 1.0 %copy-done.1 = bf16[64,3,9,128]{3,0,2,1:T(8,128)(2,1)S(1)} copy-done((bf16[64,3,9,128]{3,0,2,1:T(8,128)(2,1)S(1)}, bf16[64,3,9,128]{3,0,2,1:T(8,128)(2,1)}, u32[]{:S(2)}) %copy-start.1) | copy-done | bytes 442392
  2.9 0.0 copy-start.2
  2.9 0.9 %copy-done.2 = bf16[256,2,90]{0,1,2:T(2,128)(2,1)S(1)} copy-done((bf16[256,2,90]{0,1,2:T(2,128)(2,1)S(1)}, bf16[256,2,90]{0,1,2:T(2,128)(2,1)}, u32[]{:S(2)}) %copy-start.2) | copy-done | bytes 92184
  3.8 0.0 copy-start.3
  3.8 0.9 %copy-done.3 = bf16[256,2,90]{0,1,2:T(2,128)(2,1)S(1)} copy-done((bf16[256,2,90]{0,1,2:T(2,128)(2,1)S(1)}, bf16[256,2,90]{0,1,2:T(2,128)(2,1)}, u32[]{:S(2)}) %copy-start.3) | copy-done | bytes 92184
  4.7 0.0 copy-start.4
  4.7 0.7 %copy-done.4 = s32[64]{0:T(128)S(1)} copy-done((s32[64]{0:T(128)S(1)}, s32[64]{0:T(128)}, u32[]{:S(2)}) %copy-start.4) | copy-done | bytes 280
  5.4 51.6 %shard_map.76 = (bf16[90,2,256]{2,1,0:T(2,128)(2,1)S(1)}, bf16[90,2,256]{2,1,0:T(2,128)(2,1)S(1)}, f32[9,128]{1,0:T(8,128)S(1)}) custom-call(bf16[90,2,256]{2,1,0:T(2,128)(2,1)S(1)} %bitcast.13, bf16[1728,128]{1,0:T(8,128)(2,1)S(1)} %bitcast.10, s32[64]{0:T(128)S(1)} %copy-done.4, bf16[9,256,256]{2,1,0:T(8,128)(2,1)S(1)} %bitcast.9, ...), custom_call_target="tpu_custom_call" | custom-call | tf_op jit(solution)/shard_map/pallas_call | solution.py:349
  57.0 0.6 %copy.11 = bf16[256,2,90]{0,1,2:T(2,128)(2,1)} copy(bf16[256,2,90]{0,1,2:T(2,128)(2,1)S(1)} %bitcast.12) | data formatting | bytes 184320
  57.6 0.6 %copy.12 = bf16[256,2,90]{0,1,2:T(2,128)(2,1)} copy(bf16[256,2,90]{0,1,2:T(2,128)(2,1)S(1)} %bitcast.11) | data formatting | bytes 184320
  58.2 0.6 %copy.13 = f32[1152]{0:T(1024)} copy(f32[1152]{0:T(1024)S(1)} %bitcast.15) | data formatting | bytes 9216
Async XLA Ops:
  0.6 1.3 %copy-start = (bf16[256,9,256]{2,0,1:T(8,128)(2,1)S(1)}, bf16[256,9,256]{2,0,1:T(8,128)(2,1)}, u32[]{:S(2)}) copy-start(bf16[256,9,256]{2,0,1:T(8,128)(2,1)} %param.8) | copy-start | bytes 3538948
  1.9 1.0 %copy-start.1 = (bf16[64,3,9,128]{3,0,2,1:T(8,128)(2,1)S(1)}, bf16[64,3,9,128]{3,0,2,1:T(8,128)(2,1)}, u32[]{:S(2)}) copy-start(bf16[64,3,9,128]{3,0,2,1:T(8,128)(2,1)} %param.6) | copy-start | bytes 1327108
  2.9 0.9 %copy-start.2 = (bf16[256,2,90]{0,1,2:T(2,128)(2,1)S(1)}, bf16[256,2,90]{0,1,2:T(2,128)(2,1)}, u32[]{:S(2)}) copy-start(bf16[256,2,90]{0,1,2:T(2,128)(2,1)} %param.5) | copy-start | bytes 276484
  3.8 0.9 %copy-start.3 = (bf16[256,2,90]{0,1,2:T(2,128)(2,1)S(1)}, bf16[256,2,90]{0,1,2:T(2,128)(2,1)}, u32[]{:S(2)}) copy-start(bf16[256,2,90]{0,1,2:T(2,128)(2,1)} %param.9) | copy-start | bytes 276484
  4.7 0.7 %copy-start.4 = (s32[64]{0:T(128)S(1)}, s32[64]{0:T(128)}, u32[]{:S(2)}) copy-start(s32[64]{0:T(128)} %hw_ref.1) | copy-start | bytes 772

commit v2 on v1

v2 whole, which is shorter than its diff:
```python
import math

import jax
import jax.numpy as jnp
from jax import lax
from jax.experimental import pallas as pl
from jax.experimental.pallas import tpu as pltpu
from jax.sharding import PartitionSpec as P

MESH = pl.DeviceIdType.MESH
BF = jnp.bfloat16
F32 = jnp.float32

CH = 256
KB = 9
JC = 90
JP = 96
HALO = 64
NLAT_AX = 32
NLON_AX = 16
NX, NZ, NY = 4, 8, 8


def iota(shape, dim):
    return lax.broadcasted_iota(jnp.int32, shape, dim)


def onehot(cond):
    return jnp.where(cond, 1.0, 0.0).astype(BF)


def mm(a, b):
    return jnp.dot(a, b, preferred_element_type=F32)


def mm_nt(a, b):
    return lax.dot_general(a, b, (((1,), (1,)), ((), ())), preferred_element_type=F32)


def kernel(
    f_hbm, basis_hbm, hw_hbm, w_hbm, c_hbm,
    out_ref, ig_ref, wg_ref,
    fv, cv, bv, hw_ref, wv,
    f_last, c_last,
    xf, xc,
    base_f, base_b, band_f, band_b, masks,
    pb, sb, cot_t,
    g_own, c_send, c_recv,
    xa_own, xa_send, xa_recv,
    zb_own, zb_send, zb_recv,
    za_f32, za_send, za_recv,
    xb_f32, xb_send, xb_recv,
    ya_f32, yb_f32, y_send, y_recv,
    in_sem, halo_ss, halo_rs, c_ss, c_rs, xa_ss, xa_rs, zb_ss, zb_rs, za_ss, za_rs, xb_ss, xb_rs, y_ss, y_rs,
):
    lat = lax.axis_index("lat")
    lon = lax.axis_index("lon")
    core = lat % 2
    zl = (lat // 2) % 4
    x = lat // 8
    zh = lon // 8
    y = lon % 8
    z = zh * 4 + zl
    i0 = lat * 2

    def dev_x(s):
        return (((x + s) % NX) * 8 + zl * 2 + core, lon)

    def dev_z(s):
        t = (z + s) % NZ
        return (x * 8 + (t % 4) * 2 + core, (t // 4) * 8 + y)

    def dev_y(s):
        return (lat, zh * 8 + (y + s) % NY)

    dev_core = (x * 8 + zl * 2 + (1 - core), lon)

    def near(up, right):
        return ((lat + NLAT_AX + up) % NLAT_AX, (lon + NLON_AX + right) % NLON_AX)

    barrier = pltpu.get_barrier_semaphore()
    peers = [near(u, r) for u in (-1, 0, 1) for r in (-1, 0, 1) if u or r]
    peers += [dev_core]
    peers += [dev_x(s) for s in range(1, NX)]
    peers += [dev_z(s) for s in range(1, NZ)]
    peers += [dev_y(s) for s in range(1, NY)]
    for peer in peers:
        pl.semaphore_signal(barrier, inc=1, device_id=peer, device_id_type=MESH)

    loads = [
        pltpu.make_async_copy(src, dst, in_sem.at[n])
        for n, (src, dst) in enumerate(
            ((f_hbm, fv), (c_hbm, cv), (basis_hbm, bv), (hw_hbm, hw_ref), (w_hbm, wv))
        )
    ]
    for load in loads:
        load.start()

    def remote(src, dst, ss, rs, dev):
        return pltpu.make_async_remote_copy(
            src_ref=src, dst_ref=dst, send_sem=ss, recv_sem=rs, device_id=dev, device_id_type=MESH
        )

    p = iota((320, 180), 0)
    r_own = (p >= JP).astype(jnp.int32)
    r_last = (p >= 256).astype(jnp.int32)
    want = jnp.where(p < 192, 2 * (p - JP * r_own) + r_own, 2 * (p - 192 - HALO * r_last + JC - HALO) + r_last)
    split = onehot(iota((320, 180), 1) == want)
    q192 = iota((180, 192), 1)
    s192 = (q192 >= JP).astype(jnp.int32)
    join_own = onehot(iota((180, 192), 0) == 2 * (q192 - JP * s192) + s192)

    def place(raw, buf, last):
        rows = mm(split, raw[...].reshape(180, CH)).astype(BF)
        buf[1, 0:JP, :] = rows[0:JP]
        buf[2, 0:JP, :] = rows[JP:192]
        last[0] = rows[192:256]
        last[1] = rows[256:320]
        for row in range(4):
            buf[row, JP:128, :] = jnp.zeros((128 - JP, CH), BF)

    both, own, first = pl.ds(1, 2), pl.ds(0, JP), pl.ds(0, HALO)
    left, right = pl.ds(128, HALO), pl.ds(192, HALO)

    def halo_copies(n, buf, last):
        moves = (
            (last, buf.at[both, left], near(0, 1)),
            (buf.at[both, first], buf.at[both, right], near(0, -1)),
            (buf.at[2, own], buf.at[0, own], near(1, 0)),
            (buf.at[1, own], buf.at[3, own], near(-1, 0)),
            (last.at[1], buf.at[0, left], near(1, 1)),
            (buf.at[2, first], buf.at[0, right], near(1, -1)),
            (last.at[0], buf.at[3, left], near(-1, 1)),
            (buf.at[1, first], buf.at[3, right], near(-1, -1)),
        )
        return [
            remote(src, dst, halo_ss.at[8 * n + m], halo_rs.at[8 * n + m], dev)
            for m, (src, dst, dev) in enumerate(moves)
        ]

    loads[0].wait()
    place(fv, xf, f_last)
    pl.semaphore_wait(barrier, len(peers))
    halo_f = halo_copies(0, xf, f_last)
    halo_c = halo_copies(1, xc, c_last)
    for copy in halo_f:
        copy.start()
    loads[1].wait()
    place(cv, xc, c_last)

    loads[2].wait()
    loads[3].wait()
    n_row = iota((64, 1), 0)
    r_row = (n_row >= 27).astype(jnp.int32)
    m_row = n_row - 27 * r_row
    d_row = (m_row >= 9).astype(jnp.int32) + (m_row >= 18).astype(jnp.int32)
    k_row = m_row - 9 * d_row
    col = iota((64, 27 * 64), 1)
    lane64 = iota((64, 128), 1)
    step = r_row + d_row
    row_of = i0 + step - 1
    outside = (row_of < 0) | (row_of > 63)
    target = (d_row * 9 + k_row) * 64 + i0 + r_row
    target = jnp.where(outside, -1, target)
    taps = mm(onehot(col == target), bv[...])
    width = jnp.where(r_row == 0, hw_ref[i0], hw_ref[i0 + 1])
    base_f[...] = jnp.where(jnp.abs(lane64 - HALO) <= width, taps, 0.0)
    target = ((2 - d_row) * 9 + k_row) * 64 + row_of
    target = jnp.where(outside, -1, target)
    taps = mm(onehot(col == target), bv[...])
    widths = [hw_ref[(i0 + 63 + s) % 64] for s in range(4)]
    width = jnp.where(
        step == 0, widths[0], jnp.where(step == 1, widths[1], jnp.where(step == 2, widths[2], widths[3]))
    )
    taps = jnp.where(jnp.abs(lane64 - HALO) <= width, taps, 0.0).astype(BF)
    turn = onehot((iota((128, 128), 0) + iota((128, 128), 1)) % 128 == 0)
    base_b[...] = mm(taps, turn)

    jj = iota((JP, 128), 0)
    ll = iota((JP, 128), 1)
    for low in range(2):
        idx = 64 + ll - jj
        masks[3 * low] = onehot((idx >= low) & (idx <= 127 + low))
        masks[3 * low + 1] = onehot((ll < HALO) & (ll - jj >= low))
        masks[3 * low + 2] = onehot((ll >= HALO) & (JC + ll - jj <= 127 + low))

    def build(base, band, low):
        def body(k, carry):
            at = pl.multiple_of(k * JP, JP)
            for r in range(2):
                for d in range(3):
                    row = base[pl.ds((r * 3 + d) * 9 + k, 1), :].astype(BF)
                    wide = jnp.broadcast_to(row, (JP, 128))
                    s0 = pltpu.roll(wide, 0, 1, stride=1, stride_axis=0)
                    s1 = pltpu.roll(s0, 64, 1)
                    s2 = pltpu.roll(s0, 38, 1)
                    band[r, pl.ds(at, JP), d * 256 : d * 256 + 128] = s1 * masks[3 * low]
                    band[r, pl.ds(at, JP), d * 256 + 128 : d * 256 + 256] = (
                        s0 * masks[3 * low + 1] + s2 * masks[3 * low + 2]
                    )
            return carry

        lax.fori_loop(0, KB, body, 0)

    build(base_f, band_f, 0)
    for copy in halo_c:
        copy.start()

    o_new = iota((256, 1), 0)
    mine = (o_new >= 128).astype(jnp.int32)
    o_in = o_new - 128 * mine
    bit = mine * core + (1 - mine) * (1 - core)
    cot_rows = jnp.concatenate([xc[1, 0:JP, :], xc[2, 0:JP, :]], axis=0)
    for n, (dx, dz) in enumerate(((o_in // 32, (o_in % 32) // 4), ((o_in % 16) // 4, o_in // 16))):
        sx = (dx + x) % NX
        sz = (dz + z) % NZ
        o_old = sx * 64 + (sz % 4) * 16 + bit * 8 + (sz // 4) * 4 + o_in % 4
        order = onehot(iota((256, 256), 1) == o_old)
        cot_t[n] = mm_nt(order, cot_rows).astype(BF)

    build(base_b, band_b, 1)

    def conv(band, buf, dst):
        for r in range(2):
            res = mm(band[r], buf[r : r + 3].reshape(768, CH)).astype(BF)
            for k in range(KB):
                dst[k, r * JP : (r + 1) * JP, :] = res[k * JP : (k + 1) * JP]

    for copy in halo_f:
        copy.wait_recv()
    conv(band_f, xf, pb)

    def core_copy(k):
        return remote(c_send.at[k], c_recv.at[k], c_ss.at[k], c_rs.at[k], dev_core)

    for g in range(3):

        def grad_body(k, carry, order=g % 2):
            part = mm(cot_t[order], pb[k])
            c_send[k] = part[0:128].astype(BF)
            core_copy(k).start()
            g_own[k] = part[128:256]
            return carry

        lax.fori_loop(3 * g, 3 * g + 3, grad_body, 0)

    def xa_copy(s, g):
        part = pl.ds(3 * g, 3)
        return remote(
            xa_send.at[s - 1, part], xa_recv.at[s - 1, part], xa_ss.at[s - 1, g], xa_rs.at[s - 1, g], dev_x(s)
        )

    def zb_copy(s):
        return remote(zb_send.at[s - 1], zb_recv.at[s - 1], zb_ss.at[s - 1], zb_rs.at[s - 1], dev_z(s))

    for g in range(3):
        for m in range(3):
            k = 3 * g + m
            core_copy(k).wait_recv()
            total = g_own[k] + c_recv[k].astype(F32)
            if g == 1:
                zb_own[m] = total[0:16]
                for s in range(1, NZ):
                    zb_send[s - 1, m] = total[16 * s : 16 * s + 16].astype(BF)
            else:
                at = 3 * (g // 2) + m
                xa_own[at] = total[0:32]
                for s in range(1, NX):
                    xa_send[s - 1, at] = total[32 * s : 32 * s + 32].astype(BF)
        if g == 1:
            for s in range(1, NZ):
                zb_copy(s).start()
        else:
            for s in range(1, NX):
                xa_copy(s, g // 2).start()

    loads[4].wait()
    mixed = mm_nt(pb[0], wv[0])
    for k in range(1, KB):
        mixed = mixed + mm_nt(pb[k], wv[k])
    out_ref[...] = mm(join_own, mixed.astype(BF)).astype(BF).reshape(JC, 2, CH)

    for copy in halo_c:
        copy.wait_recv()
    conv(band_b, xc, sb)
    grad = mm(sb[0], wv[0])
    for k in range(1, KB):
        grad = grad + mm(sb[k], wv[k])
    ig_ref[...] = mm(join_own, grad.astype(BF)).astype(BF).reshape(JC, 2, CH)

    def za_copy(s):
        return remote(za_send.at[s - 1], za_recv.at[s - 1], za_ss.at[s - 1], za_rs.at[s - 1], dev_z(s))

    def xb_copy(s):
        return remote(xb_send.at[s - 1], xb_recv.at[s - 1], xb_ss.at[s - 1], xb_rs.at[s - 1], dev_x(s))

    for g in range(2):
        for s in range(1, NX):
            xa_copy(s, g).wait_recv()
        for at in range(3 * g, 3 * g + 3):
            total = xa_own[at]
            for s in range(1, NX):
                total = total + xa_recv[s - 1, at].astype(F32)
            for h in range(2):
                za_f32[pl.ds(2 * at + h, 32, stride=12), :] = total[:, 128 * h : 128 * h + 128]
    for s in range(1, NZ):
        za_send[s - 1] = za_f32[48 * s : 48 * s + 48, :].astype(BF)
        za_copy(s).start()
    for s in range(1, NZ):
        zb_copy(s).wait_recv()
    for m in range(3):
        total = zb_own[m]
        for s in range(1, NZ):
            total = total + zb_recv[s - 1, m].astype(F32)
        for h in range(2):
            xb_f32[pl.ds(2 * m + h, 16, stride=6), :] = total[:, 128 * h : 128 * h + 128]
    for s in range(1, NX):
        xb_send[s - 1, 0:24, :] = xb_f32[24 * s : 24 * s + 24, :].astype(BF)
        xb_send[s - 1, 24:32, :] = jnp.zeros((8, 128), BF)
        xb_copy(s).start()

    def y_copy(s):
        return remote(y_send.at[s - 1], y_recv.at[s - 1], y_ss.at[s - 1], y_rs.at[s - 1], dev_y(s))

    total = xb_f32[0:24, :]
    for s in range(1, NX):
        xb_copy(s).wait_recv()
        total = total + xb_recv[s - 1, 0:24, :].astype(F32)
    yb_f32[...] = total
    total = za_f32[0:48, :]
    for s in range(1, NZ):
        za_copy(s).wait_recv()
        total = total + za_recv[s - 1].astype(F32)
    ya_f32[...] = total

    def y_rows(to):
        return [ya_f32[pl.ds(6 * to, 6), :], yb_f32[pl.ds(3 * to, 3), :]]

    for s in range(1, NY):
        rows = y_rows((y + s) % NY)
        y_send[s - 1] = jnp.concatenate(rows + [jnp.zeros((7, 128), F32)], axis=0).astype(BF)
        y_copy(s).start()
    total = jnp.concatenate(y_rows(y), axis=0)
    for s in range(1, NY):
        y_copy(s).wait_recv()
        total = total + y_recv[s - 1].astype(F32)[0:9]
    total = jnp.where(y % 2 == 0, total, jnp.concatenate([total[6:9], total[0:6]], axis=0))
    wg_ref[...] = total * (1.0 / math.sqrt(2 * NLAT_AX * JC * NLON_AX))

    for copy in halo_f + halo_c:
        copy.wait_send()
    for k in range(KB):
        core_copy(k).wait_send()
    for s in range(1, NX):
        xa_copy(s, 0).wait_send()
        xa_copy(s, 1).wait_send()
        xb_copy(s).wait_send()
    for s in range(1, NZ):
        zb_copy(s).wait_send()
        za_copy(s).wait_send()
    for s in range(1, NY):
        y_copy(s).wait_send()


def local(fields, basis, half_width, weight, cotangent):
    dma = pltpu.SemaphoreType.DMA
    vmem = pltpu.VMEM
    hbm_spec = pl.BlockSpec(memory_space=pltpu.HBM)
    vm_spec = pl.BlockSpec(memory_space=pltpu.VMEM)
    shapes = (
        jax.ShapeDtypeStruct((JC, 2, CH), BF),
        jax.ShapeDtypeStruct((JC, 2, CH), BF),
        jax.ShapeDtypeStruct((9, 128), F32),
    )
    results = pl.pallas_call(
        kernel,
        out_shape=shapes,
        in_specs=[hbm_spec] * 5,
        out_specs=(vm_spec,) * 3,
        scratch_shapes=[
            vmem((JC, 2, CH), BF), vmem((JC, 2, CH), BF), vmem((27 * 64, 128), BF),
            pltpu.SMEM((64,), jnp.int32), vmem((KB, CH, CH), BF),
            vmem((2, HALO, CH), BF), vmem((2, HALO, CH), BF),
            vmem((4, 256, CH), BF), vmem((4, 256, CH), BF),
            vmem((64, 128), F32), vmem((64, 128), F32),
            vmem((2, KB * JP, 768), BF), vmem((2, KB * JP, 768), BF), vmem((6, JP, 128), BF),
            vmem((KB, 2 * JP, CH), BF), vmem((KB, 2 * JP, CH), BF), vmem((2, CH, 2 * JP), BF),
            vmem((KB, 128, CH), F32), vmem((KB, 128, CH), BF), vmem((KB, 128, CH), BF),
            vmem((6, 32, CH), F32), vmem((3, 6, 32, CH), BF), vmem((3, 6, 32, CH), BF),
            vmem((3, 16, CH), F32), vmem((7, 3, 16, CH), BF), vmem((7, 3, 16, CH), BF),
            vmem((32 * 12, 128), F32), vmem((7, 48, 128), BF), vmem((7, 48, 128), BF),
            vmem((16 * 6, 128), F32), vmem((3, 32, 128), BF), vmem((3, 32, 128), BF),
            vmem((48, 128), F32), vmem((24, 128), F32), vmem((7, 16, 128), BF), vmem((7, 16, 128), BF),
            dma((5,)), dma((16,)), dma((16,)), dma((KB,)), dma((KB,)), dma((3, 2)), dma((3, 2)),
            dma((7,)), dma((7,)), dma((7,)), dma((7,)), dma((3,)), dma((3,)), dma((7,)), dma((7,)),
        ],
        compiler_params=pltpu.CompilerParams(
            collective_id=0, has_side_effects=True, vmem_limit_bytes=48 * 1024 * 1024
        ),
    )(
        *[
            pltpu.with_memory_space_constraint(a, pltpu.HBM)
            for a in (
                jnp.transpose(fields, (2, 1, 0)),
                jnp.transpose(basis, (1, 2, 0, 3)).reshape(27 * 64, 128),
                half_width,
                jnp.transpose(weight, (1, 0, 2)),
                jnp.transpose(cotangent, (2, 1, 0)),
            )
        ]
    )
    out, ig, wg = results
    return jnp.transpose(out, (2, 1, 0)), jnp.transpose(ig, (2, 1, 0)), wg.reshape(-1)


def solution(mesh):
    placed = (P(None, "lat", "lon"), P(), P(), P(), P(None, "lat", "lon"))
    return jax.shard_map(
        local,
        mesh=mesh,
        in_specs=placed,
        out_specs=(P(None, "lat", "lon"), P(None, "lat", "lon"), P(("lat", "lon"))),
        check_vma=False,
    )
```

time: 59.1 us -> 52.4 us (0.89)
  local copies, waits for them, and re-layouts: 6.59 us -> 1.88 us
  Pallas kernels: 51.6 us -> 49.8 us
    unnamed x13 -> x3, local copies, waits for them, and re-layouts: 6.59 us -> 1.88 us
    pallas_call x1, Pallas kernels: 51.6 us -> 49.8 us  [local(): pl.pallas_call(kernel, out_shape=shapes, in_specs=[hbm_spec] * 5, out_spe...]
where the time goes in v2:
time: 52.4 us; the launch traced here: 52.3 us
  Pallas kernels  49.8 us (95%)
  local copies, waits for them, and re-layouts  1.88 us (4%)
  between operations  0.64 us (1%)
    pallas_call x1, Pallas kernels, local(): pl.pallas_call(kernel, out_shape=shapes, in_specs=[hbm_spec] * 5, out_spe...  49.8 us
    unnamed x3, local copies, waits for them, and re-layouts  1.88 us

profile of v2, /device:TPU:8, one launch (start us, length us, event | category | flops | bytes accessed | tf_op | source)
XLA Modules:
  0.0 52.3 jit_solution(9507458108657767049)
XLA Ops:
  0.6 49.8 %shard_map.76 = (bf16[90,2,256]{2,1,0:T(2,128)(2,1)S(1)}, bf16[90,2,256]{2,1,0:T(2,128)(2,1)S(1)}, f32[9,128]{1,0:T(8,128)S(1)}) custom-call(bf16[90,2,256]{2,1,0:T(2,128)(2,1)} %bitcast.14, bf16[1728,128]{1,0:T(8,128)(2,1)} %bitcast.13, s32[64]{0:T(128)} %hw_hbm.1, bf16[9,256,256]{2,1,0:T(8,128)(2,1)} %bitcast.12, bf16[90,2,256]{2,1,0:T(2,128)(2,1)} %bitcast.15), custom_call_target="tpu_custom_call" | custom-call | tf_op jit(solution)/shard_map/pallas_call | solution.py:375
  50.4 0.6 %copy.11 = bf16[256,2,90]{0,1,2:T(2,128)(2,1)} copy(bf16[256,2,90]{0,1,2:T(2,128)(2,1)S(1)} %bitcast.10) | data formatting | bytes 184320
  51.1 0.6 %copy.12 = bf16[256,2,90]{0,1,2:T(2,128)(2,1)} copy(bf16[256,2,90]{0,1,2:T(2,128)(2,1)S(1)} %bitcast.9) | data formatting | bytes 184320
  51.7 0.6 %copy.13 = f32[1152]{0:T(1024)} copy(f32[1152]{0:T(1024)S(1)} %bitcast.11) | data formatting | bytes 9216

commit v3 on v2

--- a/solution.py
+++ b/solution.py
@@ -19,6 +19,10 @@
 NLAT_AX = 32
 NLON_AX = 16
 NX, NZ, NY = 4, 8, 8
+FAR4 = (2, 1, 3)
+FAR8 = (4, 3, 5, 2, 6, 1, 7)
+NEAR4 = FAR4[::-1]
+NEAR8 = FAR8[::-1]
 
 
 def iota(shape, dim):
@@ -39,7 +43,7 @@
 
 def kernel(
     f_hbm, basis_hbm, hw_hbm, w_hbm, c_hbm,
-    out_ref, ig_ref, wg_ref,
+    both_ref, wg_ref,
     fv, cv, bv, hw_ref, wv,
     f_last, c_last,
     xf, xc,
@@ -120,7 +124,7 @@
             buf[row, JP:128, :] = jnp.zeros((128 - JP, CH), BF)
 
     both, own, first = pl.ds(1, 2), pl.ds(0, JP), pl.ds(0, HALO)
-    left, right = pl.ds(128, HALO), pl.ds(192, HALO)
+    left, right, sides = pl.ds(128, HALO), pl.ds(192, HALO), pl.ds(128, 2 * HALO)
 
     def halo_copies(n, buf, last):
         moves = (
@@ -128,11 +132,19 @@
             (buf.at[both, first], buf.at[both, right], near(0, -1)),
             (buf.at[2, own], buf.at[0, own], near(1, 0)),
             (buf.at[1, own], buf.at[3, own], near(-1, 0)),
-            (last.at[1], buf.at[0, left], near(1, 1)),
-            (buf.at[2, first], buf.at[0, right], near(1, -1)),
-            (last.at[0], buf.at[3, left], near(-1, 1)),
-            (buf.at[1, first], buf.at[3, right], near(-1, -1)),
         )
+        if n == 0:
+            moves += (
+                (last.at[1], buf.at[0, left], near(1, 1)),
+                (buf.at[2, first], buf.at[0, right], near(1, -1)),
+                (last.at[0], buf.at[3, left], near(-1, 1)),
+                (buf.at[1, first], buf.at[3, right], near(-1, -1)),
+            )
+        else:
+            moves += (
+                (buf.at[2, sides], buf.at[0, sides], near(1, 0)),
+                (buf.at[1, sides], buf.at[3, sides], near(-1, 0)),
+            )
         return [
             remote(src, dst, halo_ss.at[8 * n + m], halo_rs.at[8 * n + m], dev)
             for m, (src, dst, dev) in enumerate(moves)
@@ -203,8 +215,6 @@
         lax.fori_loop(0, KB, body, 0)
 
     build(base_f, band_f, 0)
-    for copy in halo_c:
-        copy.start()
 
     o_new = iota((256, 1), 0)
     mine = (o_new >= 128).astype(jnp.int32)
@@ -228,21 +238,21 @@
 
     for copy in halo_f:
         copy.wait_recv()
+    for copy in halo_c[:4]:
+        copy.start()
     conv(band_f, xf, pb)
 
-    def core_copy(k):
-        return remote(c_send.at[k], c_recv.at[k], c_ss.at[k], c_rs.at[k], dev_core)
+    def core_copy(g):
+        part = pl.ds(3 * g, 3)
+        return remote(c_send.at[part], c_recv.at[part], c_ss.at[g], c_rs.at[g], dev_core)
 
     for g in range(3):
-
-        def grad_body(k, carry, order=g % 2):
-            part = mm(cot_t[order], pb[k])
-            c_send[k] = part[0:128].astype(BF)
-            core_copy(k).start()
-            g_own[k] = part[128:256]
-            return carry
-
-        lax.fori_loop(3 * g, 3 * g + 3, grad_body, 0)
+        parts = [mm(cot_t[g % 2], pb[k]) for k in range(3 * g, 3 * g + 3)]
+        for m, part in enumerate(parts):
+            c_send[3 * g + m] = part[0:128].astype(BF)
+        core_copy(g).start()
+        for m, part in enumerate(parts):
+            g_own[3 * g + m] = part[128:256]
 
     def xa_copy(s, g):
         part = pl.ds(3 * g, 3)
@@ -254,9 +264,9 @@
         return remote(zb_send.at[s - 1], zb_recv.at[s - 1], zb_ss.at[s - 1], zb_rs.at[s - 1], dev_z(s))
 
     for g in range(3):
+        core_copy(g).wait_recv()
         for m in range(3):
             k = 3 * g + m
-            core_copy(k).wait_recv()
             total = g_own[k] + c_recv[k].astype(F32)
             if g == 1:
                 zb_own[m] = total[0:16]
@@ -268,25 +278,17 @@
                 for s in range(1, NX):
                     xa_send[s - 1, at] = total[32 * s : 32 * s + 32].astype(BF)
         if g == 1:
-            for s in range(1, NZ):
+            for s in FAR8:
                 zb_copy(s).start()
         else:
-            for s in range(1, NX):
+            for s in FAR4:
                 xa_copy(s, g // 2).start()
 
     loads[4].wait()
     mixed = mm_nt(pb[0], wv[0])
     for k in range(1, KB):
         mixed = mixed + mm_nt(pb[k], wv[k])
-    out_ref[...] = mm(join_own, mixed.astype(BF)).astype(BF).reshape(JC, 2, CH)
-
-    for copy in halo_c:
-        copy.wait_recv()
-    conv(band_b, xc, sb)
-    grad = mm(sb[0], wv[0])
-    for k in range(1, KB):
-        grad = grad + mm(sb[k], wv[k])
-    ig_ref[...] = mm(join_own, grad.astype(BF)).astype(BF).reshape(JC, 2, CH)
+    both_ref[0] = mm(join_own, mixed.astype(BF)).astype(BF).reshape(JC, 2, CH)
 
     def za_copy(s):
         return remote(za_send.at[s - 1], za_recv.at[s - 1], za_ss.at[s - 1], za_rs.at[s - 1], dev_z(s))
@@ -303,7 +305,7 @@
                 total = total + xa_recv[s - 1, at].astype(F32)
             for h in range(2):
                 za_f32[pl.ds(2 * at + h, 32, stride=12), :] = total[:, 128 * h : 128 * h + 128]
-    for s in range(1, NZ):
+    for s in FAR8:
         za_send[s - 1] = za_f32[48 * s : 48 * s + 48, :].astype(BF)
         za_copy(s).start()
     for s in range(1, NZ):
@@ -314,7 +316,7 @@
             total = total + zb_recv[s - 1, m].astype(F32)
         for h in range(2):
             xb_f32[pl.ds(2 * m + h, 16, stride=6), :] = total[:, 128 * h : 128 * h + 128]
-    for s in range(1, NX):
+    for s in FAR4:
         xb_send[s - 1, 0:24, :] = xb_f32[24 * s : 24 * s + 24, :].astype(BF)
         xb_send[s - 1, 24:32, :] = jnp.zeros((8, 128), BF)
         xb_copy(s).start()
@@ -322,13 +324,18 @@
     def y_copy(s):
         return remote(y_send.at[s - 1], y_recv.at[s - 1], y_ss.at[s - 1], y_rs.at[s - 1], dev_y(s))
 
+    for copy in halo_c[:4]:
+        copy.wait_recv()
+    for copy in halo_c[4:]:
+        copy.start()
+
     total = xb_f32[0:24, :]
-    for s in range(1, NX):
+    for s in NEAR4:
         xb_copy(s).wait_recv()
         total = total + xb_recv[s - 1, 0:24, :].astype(F32)
     yb_f32[...] = total
     total = za_f32[0:48, :]
-    for s in range(1, NZ):
+    for s in NEAR8:
         za_copy(s).wait_recv()
         total = total + za_recv[s - 1].astype(F32)
     ya_f32[...] = total
@@ -336,12 +343,20 @@
     def y_rows(to):
         return [ya_f32[pl.ds(6 * to, 6), :], yb_f32[pl.ds(3 * to, 3), :]]
 
-    for s in range(1, NY):
+    for s in FAR8:
         rows = y_rows((y + s) % NY)
         y_send[s - 1] = jnp.concatenate(rows + [jnp.zeros((7, 128), F32)], axis=0).astype(BF)
         y_copy(s).start()
+    for copy in halo_c[4:]:
+        copy.wait_recv()
+    conv(band_b, xc, sb)
+    grad = mm(sb[0], wv[0])
+    for k in range(1, KB):
+        grad = grad + mm(sb[k], wv[k])
+    both_ref[1] = mm(join_own, grad.astype(BF)).astype(BF).reshape(JC, 2, CH)
+
     total = jnp.concatenate(y_rows(y), axis=0)
-    for s in range(1, NY):
+    for s in NEAR8:
         y_copy(s).wait_recv()
         total = total + y_recv[s - 1].astype(F32)[0:9]
     total = jnp.where(y % 2 == 0, total, jnp.concatenate([total[6:9], total[0:6]], axis=0))
@@ -349,8 +364,8 @@
 
     for copy in halo_f + halo_c:
         copy.wait_send()
-    for k in range(KB):
-        core_copy(k).wait_send()
+    for g in range(3):
+        core_copy(g).wait_send()
     for s in range(1, NX):
         xa_copy(s, 0).wait_send()
         xa_copy(s, 1).wait_send()
@@ -367,16 +382,11 @@
     vmem = pltpu.VMEM
     hbm_spec = pl.BlockSpec(memory_space=pltpu.HBM)
     vm_spec = pl.BlockSpec(memory_space=pltpu.VMEM)
-    shapes = (
-        jax.ShapeDtypeStruct((JC, 2, CH), BF),
-        jax.ShapeDtypeStruct((JC, 2, CH), BF),
-        jax.ShapeDtypeStruct((9, 128), F32),
-    )
-    results = pl.pallas_call(
+    both, wg = pl.pallas_call(
         kernel,
-        out_shape=shapes,
+        out_shape=(jax.ShapeDtypeStruct((2, JC, 2, CH), BF), jax.ShapeDtypeStruct((9, 128), F32)),
         in_specs=[hbm_spec] * 5,
-        out_specs=(vm_spec,) * 3,
+        out_specs=(vm_spec,) * 2,
         scratch_shapes=[
             vmem((JC, 2, CH), BF), vmem((JC, 2, CH), BF), vmem((27 * 64, 128), BF),
             pltpu.SMEM((64,), jnp.int32), vmem((KB, CH, CH), BF),
@@ -391,7 +401,7 @@
             vmem((32 * 12, 128), F32), vmem((7, 48, 128), BF), vmem((7, 48, 128), BF),
             vmem((16 * 6, 128), F32), vmem((3, 32, 128), BF), vmem((3, 32, 128), BF),
             vmem((48, 128), F32), vmem((24, 128), F32), vmem((7, 16, 128), BF), vmem((7, 16, 128), BF),
-            dma((5,)), dma((16,)), dma((16,)), dma((KB,)), dma((KB,)), dma((3, 2)), dma((3, 2)),
+            dma((5,)), dma((16,)), dma((16,)), dma((3,)), dma((3,)), dma((3, 2)), dma((3, 2)),
             dma((7,)), dma((7,)), dma((7,)), dma((7,)), dma((3,)), dma((3,)), dma((7,)), dma((7,)),
         ],
         compiler_params=pltpu.CompilerParams(
@@ -409,8 +419,7 @@
             )
         ]
     )
-    out, ig, wg = results
-    return jnp.transpose(out, (2, 1, 0)), jnp.transpose(ig, (2, 1, 0)), wg.reshape(-1)
+    return jnp.transpose(both[0], (2, 1, 0)), jnp.transpose(both[1], (2, 1, 0)), wg.reshape(-1)
 
 
 def solution(mesh):

time: 52.4 us -> 45.1 us (0.86)
  Pallas kernels: 49.8 us -> 43 us
    pallas_call x1, Pallas kernels: 49.8 us -> 43 us  [local(): pl.pallas_call(kernel, out_shape=(jax.ShapeDtypeStruct((2, JC, 2, CH), BF...]
    unnamed x3 -> x1, local copies, waits for them, and re-layouts: 1.88 us -> 0.6 us
    transpose x0 -> x1, local copies, waits for them, and re-layouts: none -> 0.8 us  [local(): jnp.transpose(both[1], (2, 1, 0))]
where the time goes in v3:
time: 45.1 us; the launch traced here: 45 us
  Pallas kernels  43 us (95%)
  local copies, waits for them, and re-layouts  1.4 us (3%)
  between operations  0.64 us (1%)
    pallas_call x1, Pallas kernels, local(): pl.pallas_call(kernel, out_shape=(jax.ShapeDtypeStruct((2, JC, 2, CH), BF...  43 us

profile of v3, /device:TPU:8, one launch (start us, length us, event | category | flops | bytes accessed | tf_op | source)
XLA Modules:
  0.0 45.0 jit_solution(6190129127134632240)
XLA Ops:
  0.6 43.0 %shard_map.76 = (bf16[2,90,2,256]{3,2,1,0:T(2,128)(2,1)S(1)}, f32[9,128]{1,0:T(8,128)S(1)}) custom-call(bf16[90,2,256]{2,1,0:T(2,128)(2,1)} %bitcast.18, bf16[1728,128]{1,0:T(8,128)(2,1)} %bitcast.17, s32[64]{0:T(128)} %hw_hbm.1, bf16[9,256,256]{2,1,0:T(8,128)(2,1)} %bitcast.16, bf16[90,2,256]{2,1,0:T(2,128)(2,1)} %bitcast.19), custom_call_target="tpu_custom_call" | custom-call | tf_op jit(solution)/shard_map/pallas_call | solution.py:385
  43.6 0.8 %slice_bitcast_fusion = (bf16[256,2,90]{0,1,2:T(2,128)(2,1)}, bf16[256,2,90]{0,1,2:T(2,128)(2,1)}) fusion(bf16[2,90,2,256]{3,2,1,0:T(2,128)(2,1)S(1)} %get-tuple-element.5), kind=kLoop, calls=%fused_computation | loop fusion | bytes 368640 | tf_op jit(solution)/shard_map/transpose | solution.py:422
  44.4 0.6 %copy.9 = f32[1152]{0:T(1024)} copy(f32[1152]{0:T(1024)S(1)} %bitcast.15) | data formatting | bytes 9216

commit v4 on v3

--- a/solution.py
+++ b/solution.py
@@ -50,12 +50,10 @@
     base_f, base_b, band_f, band_b, masks,
     pb, sb, cot_t,
     g_own, c_send, c_recv,
-    xa_own, xa_send, xa_recv,
-    zb_own, zb_send, zb_recv,
-    za_f32, za_send, za_recv,
-    xb_f32, xb_send, xb_recv,
-    ya_f32, yb_f32, y_send, y_recv,
-    in_sem, halo_ss, halo_rs, c_ss, c_rs, xa_ss, xa_rs, zb_ss, zb_rs, za_ss, za_rs, xb_ss, xb_rs, y_ss, y_rs,
+    x_own, x_send, x_recv,
+    z_f32, z_send, z_recv,
+    y_f32, y_send, y_recv,
+    in_sem, halo_ss, halo_rs, c_ss, c_rs, x_ss, x_rs, z_ss, z_rs, y_ss, y_rs,
 ):
     lat = lax.axis_index("lat")
     lon = lax.axis_index("lon")
@@ -83,11 +81,12 @@
         return ((lat + NLAT_AX + up) % NLAT_AX, (lon + NLON_AX + right) % NLON_AX)
 
     barrier = pltpu.get_barrier_semaphore()
-    peers = [near(u, r) for u in (-1, 0, 1) for r in (-1, 0, 1) if u or r]
+    peers = [near(u, r) for r in (-1, 1) for u in (-1, 0, 1)]
+    for s in FAR8:
+        peers += [dev_z(s), dev_y(s)]
+    peers += [near(-1, 0), near(1, 0)]
+    peers += [dev_x(s) for s in FAR4]
     peers += [dev_core]
-    peers += [dev_x(s) for s in range(1, NX)]
-    peers += [dev_z(s) for s in range(1, NZ)]
-    peers += [dev_y(s) for s in range(1, NY)]
     for peer in peers:
         pl.semaphore_signal(barrier, inc=1, device_id=peer, device_id_type=MESH)
 
@@ -217,16 +216,14 @@
     build(base_f, band_f, 0)
 
     o_new = iota((256, 1), 0)
-    mine = (o_new >= 128).astype(jnp.int32)
-    o_in = o_new - 128 * mine
-    bit = mine * core + (1 - mine) * (1 - core)
+    mine = (o_new % 64) // 32
+    to_x = ((o_new % 32) // 8 + x) % NX
+    to_z = 2 * (o_new // 64) + (o_new % 8) // 4
+    to_core = mine * core + (1 - mine) * (1 - core)
+    o_old = to_x * 64 + (to_z % 4) * 16 + to_core * 8 + (to_z // 4) * 4 + o_new % 4
+    order = onehot(iota((256, 256), 1) == o_old)
     cot_rows = jnp.concatenate([xc[1, 0:JP, :], xc[2, 0:JP, :]], axis=0)
-    for n, (dx, dz) in enumerate(((o_in // 32, (o_in % 32) // 4), ((o_in % 16) // 4, o_in // 16))):
-        sx = (dx + x) % NX
-        sz = (dz + z) % NZ
-        o_old = sx * 64 + (sz % 4) * 16 + bit * 8 + (sz // 4) * 4 + o_in % 4
-        order = onehot(iota((256, 256), 1) == o_old)
-        cot_t[n] = mm_nt(order, cot_rows).astype(BF)
+    cot_t[...] = mm_nt(order, cot_rows).astype(BF)
 
     build(base_b, band_b, 1)
 
@@ -242,47 +239,37 @@
         copy.start()
     conv(band_f, xf, pb)
 
-    def core_copy(g):
-        part = pl.ds(3 * g, 3)
-        return remote(c_send.at[part], c_recv.at[part], c_ss.at[g], c_rs.at[g], dev_core)
-
-    for g in range(3):
-        parts = [mm(cot_t[g % 2], pb[k]) for k in range(3 * g, 3 * g + 3)]
-        for m, part in enumerate(parts):
-            c_send[3 * g + m] = part[0:128].astype(BF)
-        core_copy(g).start()
-        for m, part in enumerate(parts):
-            g_own[3 * g + m] = part[128:256]
-
-    def xa_copy(s, g):
-        part = pl.ds(3 * g, 3)
-        return remote(
-            xa_send.at[s - 1, part], xa_recv.at[s - 1, part], xa_ss.at[s - 1, g], xa_rs.at[s - 1, g], dev_x(s)
-        )
-
-    def zb_copy(s):
-        return remote(zb_send.at[s - 1], zb_recv.at[s - 1], zb_ss.at[s - 1], zb_rs.at[s - 1], dev_z(s))
-
-    for g in range(3):
-        core_copy(g).wait_recv()
-        for m in range(3):
-            k = 3 * g + m
-            total = g_own[k] + c_recv[k].astype(F32)
-            if g == 1:
-                zb_own[m] = total[0:16]
-                for s in range(1, NZ):
-                    zb_send[s - 1, m] = total[16 * s : 16 * s + 16].astype(BF)
-            else:
-                at = 3 * (g // 2) + m
-                xa_own[at] = total[0:32]
-                for s in range(1, NX):
-                    xa_send[s - 1, at] = total[32 * s : 32 * s + 32].astype(BF)
-        if g == 1:
-            for s in FAR8:
-                zb_copy(s).start()
-        else:
-            for s in FAR4:
-                xa_copy(s, g // 2).start()
+    def core_copy(q):
+        return remote(c_send.at[q], c_recv.at[q], c_ss.at[q], c_rs.at[q], dev_core)
+
+    def x_copy(q, s):
+        return remote(x_send.at[q, s - 1], x_recv.at[q, s - 1], x_ss.at[q, s - 1], x_rs.at[q, s - 1], dev_x(s))
+
+    def grad_part(q):
+        parts = [mm(cot_t[64 * q : 64 * q + 64], pb[k]) for k in range(KB)]
+        for k, part in enumerate(parts):
+            c_send[q, k] = part[0:32].astype(BF)
+        core_copy(q).start()
+        for k, part in enumerate(parts):
+            g_own[q, k] = part[32:64]
+
+    def core_sum(q):
+        core_copy(q).wait_recv()
+        totals = [g_own[q, k] + c_recv[q, k].astype(F32) for k in range(KB)]
+        for s in FAR4:
+            rows = [total[8 * s : 8 * s + 8] for total in totals] + [jnp.zeros((8, CH), F32)]
+            x_send[q, s - 1] = jnp.concatenate(rows, axis=0).astype(BF)
+            x_copy(q, s).start()
+        x_own[q] = jnp.concatenate([total[0:8] for total in totals], axis=0)
+
+    grad_part(0)
+    grad_part(1)
+    core_sum(0)
+    grad_part(2)
+    core_sum(1)
+    grad_part(3)
+    core_sum(2)
+    core_sum(3)
 
     loads[4].wait()
     mixed = mm_nt(pb[0], wv[0])
@@ -290,62 +277,50 @@
         mixed = mixed + mm_nt(pb[k], wv[k])
     both_ref[0] = mm(join_own, mixed.astype(BF)).astype(BF).reshape(JC, 2, CH)
 
-    def za_copy(s):
-        return remote(za_send.at[s - 1], za_recv.at[s - 1], za_ss.at[s - 1], za_rs.at[s - 1], dev_z(s))
-
-    def xb_copy(s):
-        return remote(xb_send.at[s - 1], xb_recv.at[s - 1], xb_ss.at[s - 1], xb_rs.at[s - 1], dev_x(s))
-
-    for g in range(2):
-        for s in range(1, NX):
-            xa_copy(s, g).wait_recv()
-        for at in range(3 * g, 3 * g + 3):
-            total = xa_own[at]
-            for s in range(1, NX):
-                total = total + xa_recv[s - 1, at].astype(F32)
+    def z_copy(to):
+        slot = (z + NZ - 1 - to) % NZ
+        dev = (x * 8 + (to % 4) * 2 + core, (to // 4) * 8 + y)
+        return remote(z_send.at[to], z_recv.at[slot], z_ss.at[to], z_rs.at[slot], dev)
+
+    def x_sum(q):
+        total = x_own[q]
+        for s in NEAR4:
+            x_copy(q, s).wait_recv()
+            total = total + x_recv[q, s - 1, 0:72, :].astype(F32)
+        for k in range(KB):
             for h in range(2):
-                za_f32[pl.ds(2 * at + h, 32, stride=12), :] = total[:, 128 * h : 128 * h + 128]
-    for s in FAR8:
-        za_send[s - 1] = za_f32[48 * s : 48 * s + 48, :].astype(BF)
-        za_copy(s).start()
-    for s in range(1, NZ):
-        zb_copy(s).wait_recv()
-    for m in range(3):
-        total = zb_own[m]
-        for s in range(1, NZ):
-            total = total + zb_recv[s - 1, m].astype(F32)
-        for h in range(2):
-            xb_f32[pl.ds(2 * m + h, 16, stride=6), :] = total[:, 128 * h : 128 * h + 128]
-    for s in FAR4:
-        xb_send[s - 1, 0:24, :] = xb_f32[24 * s : 24 * s + 24, :].astype(BF)
-        xb_send[s - 1, 24:32, :] = jnp.zeros((8, 128), BF)
-        xb_copy(s).start()
-
-    def y_copy(s):
-        return remote(y_send.at[s - 1], y_recv.at[s - 1], y_ss.at[s - 1], y_rs.at[s - 1], dev_y(s))
-
+                z_f32[q, pl.ds(2 * k + h, 8, stride=18), :] = total[8 * k : 8 * k + 8, 128 * h : 128 * h + 128]
+        for to in (2 * q, 2 * q + 1):
+            at = 72 * (to % 2)
+            z_send[to, 0:72, :] = z_f32[q, at : at + 72, :].astype(BF)
+            z_send[to, 72:80, :] = jnp.zeros((8, 128), BF)
+
+            @pl.when(z != to)
+            def _(to=to):
+                z_copy(to).start()
+
+    x_sum(0)
+    x_sum(1)
     for copy in halo_c[:4]:
         copy.wait_recv()
     for copy in halo_c[4:]:
         copy.start()
 
-    total = xb_f32[0:24, :]
-    for s in NEAR4:
-        xb_copy(s).wait_recv()
-        total = total + xb_recv[s - 1, 0:24, :].astype(F32)
-    yb_f32[...] = total
-    total = za_f32[0:48, :]
+    x_sum(2)
+    x_sum(3)
+
+    def y_copy(s):
+        return remote(y_send.at[s - 1], y_recv.at[s - 1], y_ss.at[s - 1], y_rs.at[s - 1], dev_y(s))
+
+    total = z_f32[z // 2, pl.ds(pl.multiple_of(72 * (z % 2), 8), 72), :]
     for s in NEAR8:
-        za_copy(s).wait_recv()
-        total = total + za_recv[s - 1].astype(F32)
-    ya_f32[...] = total
-
-    def y_rows(to):
-        return [ya_f32[pl.ds(6 * to, 6), :], yb_f32[pl.ds(3 * to, 3), :]]
+        remote(z_send.at[0], z_recv.at[s - 1], z_ss.at[0], z_rs.at[s - 1], dev_z(s)).wait_recv()
+        total = total + z_recv[s - 1, 0:72, :].astype(F32)
+    y_f32[...] = total
 
     for s in FAR8:
-        rows = y_rows((y + s) % NY)
-        y_send[s - 1] = jnp.concatenate(rows + [jnp.zeros((7, 128), F32)], axis=0).astype(BF)
+        rows = y_f32[pl.ds(9 * ((y + s) % NY), 9), :]
+        y_send[s - 1] = jnp.concatenate([rows, jnp.zeros((7, 128), F32)], axis=0).astype(BF)
         y_copy(s).start()
     for copy in halo_c[4:]:
         copy.wait_recv()
@@ -355,24 +330,24 @@
         grad = grad + mm(sb[k], wv[k])
     both_ref[1] = mm(join_own, grad.astype(BF)).astype(BF).reshape(JC, 2, CH)
 
-    total = jnp.concatenate(y_rows(y), axis=0)
+    total = y_f32[pl.ds(9 * y, 9), :]
     for s in NEAR8:
         y_copy(s).wait_recv()
         total = total + y_recv[s - 1].astype(F32)[0:9]
-    total = jnp.where(y % 2 == 0, total, jnp.concatenate([total[6:9], total[0:6]], axis=0))
     wg_ref[...] = total * (1.0 / math.sqrt(2 * NLAT_AX * JC * NLON_AX))
 
     for copy in halo_f + halo_c:
         copy.wait_send()
-    for g in range(3):
-        core_copy(g).wait_send()
-    for s in range(1, NX):
-        xa_copy(s, 0).wait_send()
-        xa_copy(s, 1).wait_send()
-        xb_copy(s).wait_send()
-    for s in range(1, NZ):
-        zb_copy(s).wait_send()
-        za_copy(s).wait_send()
+    for q in range(4):
+        core_copy(q).wait_send()
+        for s in range(1, NX):
+            x_copy(q, s).wait_send()
+    for to in range(NZ):
+
+        @pl.when(z != to)
+        def _(to=to):
+            z_copy(to).wait_send()
+
     for s in range(1, NY):
         y_copy(s).wait_send()
 
@@ -394,15 +369,13 @@
             vmem((4, 256, CH), BF), vmem((4, 256, CH), BF),
             vmem((64, 128), F32), vmem((64, 128), F32),
             vmem((2, KB * JP, 768), BF), vmem((2, KB * JP, 768), BF), vmem((6, JP, 128), BF),
-            vmem((KB, 2 * JP, CH), BF), vmem((KB, 2 * JP, CH), BF), vmem((2, CH, 2 * JP), BF),
-            vmem((KB, 128, CH), F32), vmem((KB, 128, CH), BF), vmem((KB, 128, CH), BF),
-            vmem((6, 32, CH), F32), vmem((3, 6, 32, CH), BF), vmem((3, 6, 32, CH), BF),
-            vmem((3, 16, CH), F32), vmem((7, 3, 16, CH), BF), vmem((7, 3, 16, CH), BF),
-            vmem((32 * 12, 128), F32), vmem((7, 48, 128), BF), vmem((7, 48, 128), BF),
-            vmem((16 * 6, 128), F32), vmem((3, 32, 128), BF), vmem((3, 32, 128), BF),
-            vmem((48, 128), F32), vmem((24, 128), F32), vmem((7, 16, 128), BF), vmem((7, 16, 128), BF),
-            dma((5,)), dma((16,)), dma((16,)), dma((3,)), dma((3,)), dma((3, 2)), dma((3, 2)),
-            dma((7,)), dma((7,)), dma((7,)), dma((7,)), dma((3,)), dma((3,)), dma((7,)), dma((7,)),
+            vmem((KB, 2 * JP, CH), BF), vmem((KB, 2 * JP, CH), BF), vmem((CH, 2 * JP), BF),
+            vmem((4, KB, 32, CH), F32), vmem((4, KB, 32, CH), BF), vmem((4, KB, 32, CH), BF),
+            vmem((4, 72, CH), F32), vmem((4, 3, 80, CH), BF), vmem((4, 3, 80, CH), BF),
+            vmem((4, 144, 128), F32), vmem((8, 80, 128), BF), vmem((8, 80, 128), BF),
+            vmem((72, 128), F32), vmem((7, 16, 128), BF), vmem((7, 16, 128), BF),
+            dma((5,)), dma((16,)), dma((16,)), dma((4,)), dma((4,)), dma((4, 3)), dma((4, 3)),
+            dma((8,)), dma((8,)), dma((7,)), dma((7,)),
         ],
         compiler_params=pltpu.CompilerParams(
             collective_id=0, has_side_effects=True, vmem_limit_bytes=48 * 1024 * 1024

time: 45.1 us -> 43.1 us (0.956)
  Pallas kernels: 43 us -> 40.9 us
    pallas_call x1, Pallas kernels: 43 us -> 40.9 us  [local(): pl.pallas_call(kernel, out_shape=(jax.ShapeDtypeStruct((2, JC, 2, CH), BF...]
where the time goes in v4:
time: 43.1 us; the launch traced here: 43 us
  Pallas kernels  40.9 us (95%)
  local copies, waits for them, and re-layouts  1.4 us (3%)
  between operations  0.64 us (1%)
    pallas_call x1, Pallas kernels, local(): pl.pallas_call(kernel, out_shape=(jax.ShapeDtypeStruct((2, JC, 2, CH), BF...  40.9 us

profile of v4, /device:TPU:8, one launch (start us, length us, event | category | flops | bytes accessed | tf_op | source)
XLA Modules:
  0.0 43.0 jit_solution(2744167890024575468)
XLA Ops:
  0.6 40.9 %shard_map.76 = (bf16[2,90,2,256]{3,2,1,0:T(2,128)(2,1)S(1)}, f32[9,128]{1,0:T(8,128)S(1)}) custom-call(bf16[90,2,256]{2,1,0:T(2,128)(2,1)} %bitcast.18, bf16[1728,128]{1,0:T(8,128)(2,1)} %bitcast.17, s32[64]{0:T(128)} %hw_hbm.1, bf16[9,256,256]{2,1,0:T(8,128)(2,1)} %bitcast.16, bf16[90,2,256]{2,1,0:T(2,128)(2,1)} %bitcast.19), custom_call_target="tpu_custom_call" | custom-call | tf_op jit(solution)/shard_map/pallas_call | solution.py:360
  41.6 0.8 %slice_bitcast_fusion = (bf16[256,2,90]{0,1,2:T(2,128)(2,1)}, bf16[256,2,90]{0,1,2:T(2,128)(2,1)}) fusion(bf16[2,90,2,256]{3,2,1,0:T(2,128)(2,1)S(1)} %get-tuple-element.5), kind=kLoop, calls=%fused_computation | loop fusion | bytes 368640 | tf_op jit(solution)/shard_map/transpose | solution.py:395
  42.4 0.6 %copy.9 = f32[1152]{0:T(1024)} copy(f32[1152]{0:T(1024)S(1)} %bitcast.15) | data formatting | bytes 9216

commit v5 on v4

--- a/solution.py
+++ b/solution.py
@@ -277,10 +277,11 @@
         mixed = mixed + mm_nt(pb[k], wv[k])
     both_ref[0] = mm(join_own, mixed.astype(BF)).astype(BF).reshape(JC, 2, CH)
 
-    def z_copy(to):
-        slot = (z + NZ - 1 - to) % NZ
-        dev = (x * 8 + (to % 4) * 2 + core, (to // 4) * 8 + y)
-        return remote(z_send.at[to], z_recv.at[slot], z_ss.at[to], z_rs.at[slot], dev)
+    def y_copy(q, s):
+        return remote(y_send.at[q, s - 1], y_recv.at[q, s - 1], y_ss.at[q, s - 1], y_rs.at[q, s - 1], dev_y(s))
+
+    def y_rows(q, to):
+        return [z_f32[q, pl.ds(9 * to, 9), :], z_f32[q, pl.ds(72 + 9 * to, 9), :]]
 
     def x_sum(q):
         total = x_own[q]
@@ -290,10 +291,26 @@
         for k in range(KB):
             for h in range(2):
                 z_f32[q, pl.ds(2 * k + h, 8, stride=18), :] = total[8 * k : 8 * k + 8, 128 * h : 128 * h + 128]
-        for to in (2 * q, 2 * q + 1):
-            at = 72 * (to % 2)
-            z_send[to, 0:72, :] = z_f32[q, at : at + 72, :].astype(BF)
-            z_send[to, 72:80, :] = jnp.zeros((8, 128), BF)
+        for s in FAR8:
+            rows = y_rows(q, (y + s) % NY) + [jnp.zeros((14, 128), F32)]
+            y_send[q, s - 1] = jnp.concatenate(rows, axis=0).astype(BF)
+            y_copy(q, s).start()
+
+    def z_copy(to):
+        slot = (z + NZ - 1 - to) % NZ
+        dev = (x * 8 + (to % 4) * 2 + core, (to // 4) * 8 + y)
+        return remote(z_send.at[to], z_recv.at[slot], z_ss.at[to], z_rs.at[slot], dev)
+
+    def y_sum(q):
+        total = jnp.concatenate(y_rows(q, y), axis=0)
+        for s in NEAR8:
+            y_copy(q, s).wait_recv()
+            total = total + y_recv[q, s - 1].astype(F32)[0:18]
+        for m in range(2):
+            to = 2 * q + m
+            rows = total[9 * m : 9 * m + 9]
+            y_f32[to, 0:9, :] = rows
+            z_send[to] = jnp.concatenate([rows, jnp.zeros((7, 128), F32)], axis=0).astype(BF)
 
             @pl.when(z != to)
             def _(to=to):
@@ -307,21 +324,12 @@
         copy.start()
 
     x_sum(2)
+    y_sum(0)
     x_sum(3)
-
-    def y_copy(s):
-        return remote(y_send.at[s - 1], y_recv.at[s - 1], y_ss.at[s - 1], y_rs.at[s - 1], dev_y(s))
-
-    total = z_f32[z // 2, pl.ds(pl.multiple_of(72 * (z % 2), 8), 72), :]
-    for s in NEAR8:
-        remote(z_send.at[0], z_recv.at[s - 1], z_ss.at[0], z_rs.at[s - 1], dev_z(s)).wait_recv()
-        total = total + z_recv[s - 1, 0:72, :].astype(F32)
-    y_f32[...] = total
-
-    for s in FAR8:
-        rows = y_f32[pl.ds(9 * ((y + s) % NY), 9), :]
-        y_send[s - 1] = jnp.concatenate([rows, jnp.zeros((7, 128), F32)], axis=0).astype(BF)
-        y_copy(s).start()
+    y_sum(1)
+    y_sum(2)
+    y_sum(3)
+
     for copy in halo_c[4:]:
         copy.wait_recv()
     conv(band_b, xc, sb)
@@ -330,10 +338,10 @@
         grad = grad + mm(sb[k], wv[k])
     both_ref[1] = mm(join_own, grad.astype(BF)).astype(BF).reshape(JC, 2, CH)
 
-    total = y_f32[pl.ds(9 * y, 9), :]
+    total = y_f32[z, 0:9, :]
     for s in NEAR8:
-        y_copy(s).wait_recv()
-        total = total + y_recv[s - 1].astype(F32)[0:9]
+        remote(z_send.at[0], z_recv.at[s - 1], z_ss.at[0], z_rs.at[s - 1], dev_z(s)).wait_recv()
+        total = total + z_recv[s - 1].astype(F32)[0:9]
     wg_ref[...] = total * (1.0 / math.sqrt(2 * NLAT_AX * JC * NLON_AX))
 
     for copy in halo_f + halo_c:
@@ -342,14 +350,13 @@
         core_copy(q).wait_send()
         for s in range(1, NX):
             x_copy(q, s).wait_send()
+        for s in range(1, NY):
+            y_copy(q, s).wait_send()
     for to in range(NZ):
 
         @pl.when(z != to)
         def _(to=to):
             z_copy(to).wait_send()
-
-    for s in range(1, NY):
-        y_copy(s).wait_send()
 
 
 def local(fields, basis, half_width, weight, cotangent):
@@ -372,10 +379,10 @@
             vmem((KB, 2 * JP, CH), BF), vmem((KB, 2 * JP, CH), BF), vmem((CH, 2 * JP), BF),
             vmem((4, KB, 32, CH), F32), vmem((4, KB, 32, CH), BF), vmem((4, KB, 32, CH), BF),
             vmem((4, 72, CH), F32), vmem((4, 3, 80, CH), BF), vmem((4, 3, 80, CH), BF),
-            vmem((4, 144, 128), F32), vmem((8, 80, 128), BF), vmem((8, 80, 128), BF),
-            vmem((72, 128), F32), vmem((7, 16, 128), BF), vmem((7, 16, 128), BF),
+            vmem((4, 144, 128), F32), vmem((8, 16, 128), BF), vmem((8, 16, 128), BF),
+            vmem((8, 16, 128), F32), vmem((4, 7, 32, 128), BF), vmem((4, 7, 32, 128), BF),
             dma((5,)), dma((16,)), dma((16,)), dma((4,)), dma((4,)), dma((4, 3)), dma((4, 3)),
-            dma((8,)), dma((8,)), dma((7,)), dma((7,)),
+            dma((8,)), dma((8,)), dma((4, 7)), dma((4, 7)),
         ],
         compiler_params=pltpu.CompilerParams(
             collective_id=0, has_side_effects=True, vmem_limit_bytes=48 * 1024 * 1024

time: 43.1 us -> 45.4 us (1.053)
  the two profiles are of different devices: /device:TPU:8 before, /device:TPU:1 now
where the time goes in v5:
time: 45.4 us; the launch traced here: 45.2 us
  Pallas kernels  43.2 us (95%)
  local copies, waits for them, and re-layouts  1.4 us (3%)
  between operations  0.64 us (1%)
    pallas_call x1, Pallas kernels, local(): pl.pallas_call(kernel, out_shape=(jax.ShapeDtypeStruct((2, JC, 2, CH), BF...  43.2 us

profile of v5, /device:TPU:1, one launch (start us, length us, event | category | flops | bytes accessed | tf_op | source)
XLA Modules:
  0.0 45.2 jit_solution(7107222160677112992)
XLA Ops:
  0.6 43.2 %shard_map.76 = (bf16[2,90,2,256]{3,2,1,0:T(2,128)(2,1)S(1)}, f32[9,128]{1,0:T(8,128)S(1)}) custom-call(bf16[90,2,256]{2,1,0:T(2,128)(2,1)} %bitcast.18, bf16[1728,128]{1,0:T(8,128)(2,1)} %bitcast.17, s32[64]{0:T(128)} %hw_hbm.1, bf16[9,256,256]{2,1,0:T(8,128)(2,1)} %bitcast.16, bf16[90,2,256]{2,1,0:T(2,128)(2,1)} %bitcast.19), custom_call_target="tpu_custom_call" | custom-call | tf_op jit(solution)/shard_map/pallas_call | solution.py:367
  43.9 0.8 %slice_bitcast_fusion = (bf16[256,2,90]{0,1,2:T(2,128)(2,1)}, bf16[256,2,90]{0,1,2:T(2,128)(2,1)}) fusion(bf16[2,90,2,256]{3,2,1,0:T(2,128)(2,1)S(1)} %get-tuple-element.5), kind=kLoop, calls=%fused_computation | loop fusion | bytes 368640 | tf_op jit(solution)/shard_map/transpose | solution.py:402
  44.7 0.6 %copy.9 = f32[1152]{0:T(1024)} copy(f32[1152]{0:T(1024)S(1)} %bitcast.15) | data formatting | bytes 9216
